TPU v7x, 512 devices: a whole 4x4x16 slice. The times are simulated.
512 devices in a mesh: slab: 16 (over y, x), pencil: 32 (over z, core).
Axes of the slice: x: 4, y: 4, z: 16, core: 2. Of those that a mesh axis runs over, the one named last changes fastest.
Arguments:
- wavefunction: float32 [256, 2, 16, 32, 256], P('pencil', None, None, 'slab'), may hold values from -6 to 6
- propagator: float32 [2, 256, 256], replicated
- lengths: int32 [32, 256], P('slab', 'pencil'), may hold values from 1 to 256, as said below
- centrifugal: float32 [3, 16], replicated, may hold values from 0.5 to 6
- channel_pairs: int32 [32, 2], replicated, may hold values from 0 to 15, as said below
- strengths: float32 [32], replicated, may hold values from 0.5 to 4
Outputs:
- evolved: float32 [256, 2, 16, 32, 256], P('pencil', None, None, 'slab')
Inputs may be any that keep to these rules, and one draw needn't show every extreme that they name: `lengths`: every draw has a row with all 256 points live. `channel_pairs`: the two channels of a pair differ; a pair may occur more than once.
All inputs are finite; a program needn't handle non-finite values.
Results may differ from a plain program's by a relative error of at most 0.0001.
Values sent between devices are 32-bit elements; how exact they have to be, the bound alone decides.
A program may use at most 64 MiB of HBM per device.

v0:
```python
import jax
import jax.numpy as jnp
from jax import lax
from jax.sharding import PartitionSpec as P

step_tau = 0.1
grid_step = 0.5
charge = 3.0
band_beta = 0.3
highest = lax.Precision.HIGHEST


def extended(array, sides, width):
    for axis, dim in sides:
        devices, length = (lax.axis_size(axis), array.shape[dim])
        up = [(i, (i + 1) % devices) for i in range(devices - 1)]
        down = [(j, i) for i, j in up]
        last = lax.slice_in_dim(array, length - width, length, axis=dim)
        initial = lax.slice_in_dim(array, 0, width, axis=dim)
        before = lax.ppermute(last, axis, up)
        after = lax.ppermute(initial, axis, down)
        array = jnp.concatenate([before, array, after], axis=dim)
    return array


def coupling_matrix(channel_pairs, strengths, channels):
    labels = jnp.arange(channels, dtype=jnp.int32)
    first_hot = (channel_pairs[:, 0:1] == labels[None, :]).astype(jnp.float32)
    second_hot = (channel_pairs[:, 1:2] == labels[None, :]).astype(jnp.float32)
    single = jnp.dot((first_hot * strengths[:, None]).T, second_hot, precision=highest)
    return single + single.T


def radial_terms(positions, weights):
    radius = grid_step * (positions.astype(jnp.float32) + 1.0)
    return -charge / radius[None, :] + weights[:, None] / (radius * radius)[None, :]


def block_matrix(propagator):
    upper = jnp.stack([propagator[0], -propagator[1]])
    lower = jnp.stack([propagator[1], propagator[0]])
    return jnp.stack([upper, lower])


def potential_step(
    current, duration, table, centrifugal, coupling, second_pos, third_pos, first_pos
):
    first_terms = radial_terms(first_pos, centrifugal[0])
    second_terms = radial_terms(second_pos, centrifugal[1])
    third_terms = radial_terms(third_pos, centrifugal[2])
    phases = duration * (
        second_terms.T[:, :, None, None]
        + third_terms[None, :, :, None]
        + first_terms[None, :, None, :]
    )
    cosine = jnp.cos(phases)[:, None]
    sine_part = jnp.sin(phases)[:, None]
    swapped = jnp.flip(current, axis=1)
    signs = jnp.array([1.0, -1.0], dtype=jnp.float32)[None, :, None, None, None]
    turned = current * cosine + signs * swapped * sine_part
    farthest = jnp.maximum(
        jnp.maximum(second_pos[:, None, None], third_pos[None, :, None]), first_pos[None, None, :]
    ).astype(jnp.float32)
    weight = (duration / (1.0 + 0.02 * farthest))[:, None, None]
    live = (first_pos[None, None, :] < table.T[:, :, None]).astype(jnp.float32)[:, None, None]
    mixed = jnp.einsum("cd,xpdyz->xpcyz", coupling, jnp.flip(turned, axis=1), precision=highest)
    return (turned + signs * weight * mixed) * live


def along_last(current, propagator):
    return jnp.einsum("xpcyk,qpjk->xqcyj", current, block_matrix(propagator), precision=highest)


def along_first(current, propagator):
    return jnp.einsum("qpjk,kpcyz->jqcyz", block_matrix(propagator), current, precision=highest)


def band_apply(padded, count):

    def plane(offset):
        return lax.slice_in_dim(padded, offset, offset + count, axis=3)

    return (
        band_beta
        * (plane(0) - 16.0 * plane(1) + 30.0 * plane(2) - 16.0 * plane(3) + plane(4))
        / 24.0
    )


def combine_band(current, first_pass, second_pass):
    signs = jnp.array([1.0, -1.0], dtype=jnp.float32)[None, :, None, None, None]
    return current + signs * jnp.flip(first_pass, axis=1) - 0.5 * second_pass


def regroup_columns(current):
    return lax.all_to_all(current, "pencil", split_axis=4, concat_axis=0, tiled=True)


def regroup_rows(current):
    return lax.all_to_all(current, "pencil", split_axis=0, concat_axis=4, tiled=True)


def extend_rim(current):
    return extended(current, (("slab", 3),), 2)


def radial_band(current):
    slab_rows = current.shape[3]
    first_pass = band_apply(extend_rim(current), slab_rows)
    second_pass = band_apply(extend_rim(first_pass), slab_rows)
    return combine_band(current, first_pass, second_pass)


def on_device(wavefunction, propagator, lengths, centrifugal, channel_pairs, strengths):
    coupling = coupling_matrix(channel_pairs, strengths, centrifugal.shape[1])
    local_width = wavefunction.shape[0]
    full_width = wavefunction.shape[4]
    slab_rows = wavefunction.shape[3]
    pencil_place = lax.axis_index("pencil")
    slab_index = lax.axis_index("slab") * slab_rows + jnp.arange(slab_rows, dtype=jnp.int32)
    own_index = pencil_place * local_width + jnp.arange(local_width, dtype=jnp.int32)
    whole_index = jnp.arange(full_width, dtype=jnp.int32)

    def row_potential(current, duration):
        return potential_step(
            current, duration, lengths, centrifugal, coupling, own_index, slab_index, whole_index
        )

    current = row_potential(wavefunction, 0.5 * step_tau)
    for sweep in range(2):
        current = along_last(current, propagator)
        current = regroup_rows(along_first(regroup_columns(current), propagator))
        current = radial_band(current)
        current = row_potential(current, step_tau if sweep == 0 else 0.5 * step_tau)
    return current


def solution(mesh):
    in_specs = (P("pencil", None, None, "slab", None), P(), P("slab", "pencil"), P(), P(), P())
    out_specs = P("pencil", None, None, "slab", None)
    return jax.shard_map(
        on_device, mesh=mesh, in_specs=in_specs, out_specs=out_specs, check_vma=False
    )
```

profile of v0, /device:TPU:24, one launch (start us, length us, event | category | flops | bytes accessed | tf_op | source)
XLA Modules:
  0.0 362.8 jit_solution(6715319654588794328)
XLA Ops:
  0.1 0.8 slice_bitcast_fusion.1
  0.8 0.8 slice_bitcast_fusion.4
  1.6 0.8 copy.88
  2.4 0.9 fusion.49
  3.6 1.1 copy.85
  4.7 1.1 slice_negate_fusion
  6.0 2.9 fusion.48
  9.0 0.8 multiply_add_fusion.2
  10.0 0.6 fusion.8
  10.6 1.1 convolution_bitcast_fusion.3
  11.7 4.5 %copy.90 = f32[8,2,16,2,256]{2,3,0,1,4:T(2,128)} copy(f32[8,2,16,2,256]{4,2,3,0,1:T(8,128)S(1)} %convolution_bitcast_fusion.3) | data formatting | bytes 1048576 | tf_op jit(solution)/shard_map/xpcyk,qpjk->xqcyj/transpose | solution.py:71
  16.2 7.3 %reshape.267 = f32[32,1,4096]{2,1,0:T(1,128)S(1)} reshape(f32[256,2,8,2,16]{4,3,2,1,0:T(2,128)} %bitcast.133) | data formatting | bytes 1048576
  23.5 49.2 %all_to_all.72 = f32[32,1,4096]{2,1,0:T(1,128)S(1)} all-to-all(f32[32,1,4096]{2,1,0:T(1,128)S(1)} %reshape.267), channel_id=1, replica_groups=mesh['slab'=16,'pencil'=32] {'pencil'}, dimensions={0} | all-to-all | bytes 1048576 | tf_op jit(solution)/shard_map/all_to_all | solution.py:96
  72.7 0.5 broadcast.464
  73.3 1.9 reduce
  75.1 6.9 %reshape.268 = f32[256,2,8,2,16]{4,3,2,1,0:T(2,128)} reshape(f32[32,4096]{1,0:T(8,128)S(1)} %reduce) | data formatting | bytes 1048576
  82.1 4.6 %copy.144 = f32[8,2,16,2,256]{2,4,3,1,0:T(8,128)S(1)} copy(f32[8,2,16,2,256]{2,3,0,1,4:T(2,128)} %bitcast.137) | data formatting | bytes 1048576 | tf_op jit(solution)/shard_map/all_to_all | solution.py:96
  86.7 2.5 copy.92
  89.2 3.7 %copy.119 = f32[256,2,16,2,8,1]{0,4,1,5,3,2:T(8,128)S(1)} copy(f32[256,2,16,2,8,1]{2,4,3,1,0,5:T(8,128)} %bitcast.139) | data formatting | bytes 1048576 | tf_op jit(solution)/shard_map/all_to_all | solution.py:96
  93.0 1.1 convolution_bitcast_fusion.2
  94.0 4.4 %copy.94 = f32[256,2,16,2,8]{2,4,3,1,0:T(8,128)} copy(f32[256,2,16,2,8]{0,4,1,3,2:T(8,128)S(1)} %convolution_bitcast_fusion.2) | data formatting | bytes 1048576 | tf_op jit(solution)/shard_map/qpjk,kpcyz->jqcyz/transpose | solution.py:75
  98.4 3.5 reshape.269
  101.9 37.2 %all_to_all.73 = f32[32,1,4096]{2,1,0:T(1,128)S(1)} all-to-all(f32[32,1,4096]{2,1,0:T(1,128)S(1)} %reshape.269), channel_id=1, replica_groups=mesh['slab'=16,'pencil'=32] {'pencil'}, dimensions={0} | all-to-all | bytes 1048576 | tf_op jit(solution)/shard_map/all_to_all | solution.py:100
  139.1 1.9 reduce.1
  141.0 2.8 reshape.270
  143.8 4.7 %copy.143 = f32[8,2,16,2,32,8]{2,5,4,3,1,0:T(8,128)} copy(f32[8,2,16,2,32,8]{2,5,3,1,0,4:T(8,128)} %bitcast.140) | data formatting | bytes 1048576 | tf_op jit(solution)/shard_map/all_to_all | solution.py:100
  148.5 2.8 copy.101
  151.3 4.8 %collective-permute-start.1 = (f32[8,2,16,2,256]{4,2,3,1,0:T(8,128)S(1)}, f32[8,2,16,2,256]{4,2,3,1,0:T(8,128)S(1)}, u32[]{:S(2)}, u32[]{:S(2)}) collective-permute-start(f32[8,2,16,2,256]{4,2,3,1,0:T(8,128)S(1)} %copy.101), channel_id=1, source_target_pairs={{32,0},{64,32},{96,64},{128,96},{160,128},{192,160},{224,192},{256... | collective-permute-start | bytes 1572872 | tf_op jit(solution)/shard_map/ppermute | solution.py:21
  156.2 1.9 collective-permute-start
  158.1 9.1 %collective-permute-done.1 = f32[8,2,16,2,256]{4,2,3,1,0:T(8,128)S(1)} collective-permute-done((f32[8,2,16,2,256]{4,2,3,1,0:T(8,128)S(1)}, f32[8,2,16,2,256]{4,2,3,1,0:T(8,128)S(1)}, u32[]{:S(2)}, u32[]{:S(2)}) %collective-permute-start.1) | collective-permute-done | bytes 524320 | tf_op jit(solution)/shard_map/ppermute | solution.py:21
  167.2 6.2 %collective-permute-done = f32[8,2,16,2,256]{4,2,3,1,0:T(8,128)S(1)} collective-permute-done((f32[8,2,16,2,256]{4,2,3,1,0:T(8,128)S(1)}, f32[8,2,16,2,256]{4,2,3,1,0:T(8,128)S(1)}, u32[]{:S(2)}, u32[]{:S(2)}) %collective-permute-start) | collective-permute-done | bytes 524320 | tf_op jit(solution)/shard_map/ppermute | solution.py:20
  173.7 1.9 collective-permute-start.3
  175.6 3.9 %collective-permute-start.2 = (f32[8,2,16,2,256]{4,2,3,1,0:T(8,128)S(1)}, f32[8,2,16,2,256]{4,2,3,1,0:T(8,128)S(1)}, u32[]{:S(2)}, u32[]{:S(2)}) collective-permute-start(f32[8,2,16,2,256]{4,2,3,1,0:T(8,128)S(1)} %get-tuple-element.7), channel_id=1, source_target_pairs={{0,32},{32,64},{64,96},{96,128},{128,160},{160,192},{192,224},{224... | collective-permute-start | bytes 1572872 | tf_op jit(solution)/shard_map/ppermute | solution.py:20
  179.5 8.4 %collective-permute-done.3 = f32[8,2,16,2,256]{4,2,3,1,0:T(8,128)S(1)} collective-permute-done((f32[8,2,16,2,256]{4,2,3,1,0:T(8,128)S(1)}, f32[8,2,16,2,256]{4,2,3,1,0:T(8,128)S(1)}, u32[]{:S(2)}, u32[]{:S(2)}) %collective-permute-start.3) | collective-permute-done | bytes 524320 | tf_op jit(solution)/shard_map/ppermute | solution.py:21
  187.9 4.0 %collective-permute-done.2 = f32[8,2,16,2,256]{4,2,3,1,0:T(8,128)S(1)} collective-permute-done((f32[8,2,16,2,256]{4,2,3,1,0:T(8,128)S(1)}, f32[8,2,16,2,256]{4,2,3,1,0:T(8,128)S(1)}, u32[]{:S(2)}, u32[]{:S(2)}) %collective-permute-start.2) | collective-permute-done | bytes 524320 | tf_op jit(solution)/shard_map/ppermute | solution.py:20
  192.5 0.6 fusion.5
  193.1 1.1 convolution_bitcast_fusion.1
  194.2 4.5 %copy.103 = f32[8,2,16,2,256]{2,3,0,1,4:T(2,128)} copy(f32[8,2,16,2,256]{4,2,3,0,1:T(8,128)S(1)} %convolution_bitcast_fusion.1) | data formatting | bytes 1048576 | tf_op jit(solution)/shard_map/xpcyk,qpjk->xqcyj/transpose | solution.py:71
  198.7 7.3 %reshape.271 = f32[32,1,4096]{2,1,0:T(1,128)S(1)} reshape(f32[256,2,8,2,16]{4,3,2,1,0:T(2,128)} %bitcast.135) | data formatting | bytes 1048576
  206.0 37.6 %all_to_all.74 = f32[32,1,4096]{2,1,0:T(1,128)S(1)} all-to-all(f32[32,1,4096]{2,1,0:T(1,128)S(1)} %reshape.271), channel_id=1, replica_groups=mesh['slab'=16,'pencil'=32] {'pencil'}, dimensions={0} | all-to-all | bytes 1048576 | tf_op jit(solution)/shard_map/all_to_all | solution.py:96
  243.6 1.9 reduce.2
  245.5 6.9 %reshape.272 = f32[256,2,8,2,16]{4,3,2,1,0:T(2,128)} reshape(f32[32,4096]{1,0:T(8,128)S(1)} %reduce.2) | data formatting | bytes 1048576
  252.4 4.6 %copy.142 = f32[8,2,16,2,256]{2,4,3,1,0:T(8,128)S(1)} copy(f32[8,2,16,2,256]{2,3,0,1,4:T(2,128)} %bitcast.142) | data formatting | bytes 1048576 | tf_op jit(solution)/shard_map/all_to_all | solution.py:96
  257.0 2.5 copy.105
  259.6 3.7 %copy.123 = f32[256,2,16,2,8,1]{0,4,1,5,3,2:T(8,128)S(1)} copy(f32[256,2,16,2,8,1]{2,4,3,1,0,5:T(8,128)} %bitcast.144) | data formatting | bytes 1048576 | tf_op jit(solution)/shard_map/all_to_all | solution.py:96
  263.3 1.1 convolution_bitcast_fusion
  264.4 4.4 %copy.107 = f32[256,2,16,2,8]{2,4,3,1,0:T(8,128)} copy(f32[256,2,16,2,8]{0,4,1,3,2:T(8,128)S(1)} %convolution_bitcast_fusion) | data formatting | bytes 1048576 | tf_op jit(solution)/shard_map/qpjk,kpcyz->jqcyz/transpose | solution.py:75
  268.7 3.5 reshape.273
  272.2 37.3 %all_to_all.75 = f32[32,1,4096]{2,1,0:T(1,128)S(1)} all-to-all(f32[32,1,4096]{2,1,0:T(1,128)S(1)} %reshape.273), channel_id=1, replica_groups=mesh['slab'=16,'pencil'=32] {'pencil'}, dimensions={0} | all-to-all | bytes 1048576 | tf_op jit(solution)/shard_map/all_to_all | solution.py:100
  309.5 1.9 reduce.3
  311.4 2.8 reshape.274
  314.2 4.7 %copy.141 = f32[8,2,16,2,32,8]{2,5,4,3,1,0:T(8,128)} copy(f32[8,2,16,2,32,8]{2,5,3,1,0,4:T(8,128)} %bitcast.145) | data formatting | bytes 1048576 | tf_op jit(solution)/shard_map/all_to_all | solution.py:100
  318.9 2.8 copy.114
  321.6 1.9 collective-permute-start.5
  323.6 3.9 %collective-permute-start.4 = (f32[8,2,16,2,256]{4,2,3,1,0:T(8,128)S(1)}, f32[8,2,16,2,256]{4,2,3,1,0:T(8,128)S(1)}, u32[]{:S(2)}, u32[]{:S(2)}) collective-permute-start(f32[8,2,16,2,256]{4,2,3,1,0:T(8,128)S(1)} %copy.114), channel_id=1, source_target_pairs={{0,32},{32,64},{64,96},{96,128},{128,160},{160,192},{192,224},{224... | collective-permute-start | bytes 1572872 | tf_op jit(solution)/shard_map/ppermute | solution.py:20
  327.5 9.6 %collective-permute-done.5 = f32[8,2,16,2,256]{4,2,3,1,0:T(8,128)S(1)} collective-permute-done((f32[8,2,16,2,256]{4,2,3,1,0:T(8,128)S(1)}, f32[8,2,16,2,256]{4,2,3,1,0:T(8,128)S(1)}, u32[]{:S(2)}, u32[]{:S(2)}) %collective-permute-start.5) | collective-permute-done | bytes 524320 | tf_op jit(solution)/shard_map/ppermute | solution.py:21
  337.1 4.0 %collective-permute-done.4 = f32[8,2,16,2,256]{4,2,3,1,0:T(8,128)S(1)} collective-permute-done((f32[8,2,16,2,256]{4,2,3,1,0:T(8,128)S(1)}, f32[8,2,16,2,256]{4,2,3,1,0:T(8,128)S(1)}, u32[]{:S(2)}, u32[]{:S(2)}) %collective-permute-start.4) | collective-permute-done | bytes 524320 | tf_op jit(solution)/shard_map/ppermute | solution.py:20
  341.3 1.9 collective-permute-start.7
  343.3 3.9 %collective-permute-start.6 = (f32[8,2,16,2,256]{4,2,3,1,0:T(8,128)S(1)}, f32[8,2,16,2,256]{4,2,3,1,0:T(8,128)S(1)}, u32[]{:S(2)}, u32[]{:S(2)}) collective-permute-start(f32[8,2,16,2,256]{4,2,3,1,0:T(8,128)S(1)} %get-tuple-element.5), channel_id=1, source_target_pairs={{0,32},{32,64},{64,96},{96,128},{128,160},{160,192},{192,224},{224... | collective-permute-start | bytes 1572872 | tf_op jit(solution)/shard_map/ppermute | solution.py:20
  347.2 8.7 %collective-permute-done.7 = f32[8,2,16,2,256]{4,2,3,1,0:T(8,128)S(1)} collective-permute-done((f32[8,2,16,2,256]{4,2,3,1,0:T(8,128)S(1)}, f32[8,2,16,2,256]{4,2,3,1,0:T(8,128)S(1)}, u32[]{:S(2)}, u32[]{:S(2)}) %collective-permute-start.7) | collective-permute-done | bytes 524320 | tf_op jit(solution)/shard_map/ppermute | solution.py:21
  355.9 4.0 %collective-permute-done.6 = f32[8,2,16,2,256]{4,2,3,1,0:T(8,128)S(1)} collective-permute-done((f32[8,2,16,2,256]{4,2,3,1,0:T(8,128)S(1)}, f32[8,2,16,2,256]{4,2,3,1,0:T(8,128)S(1)}, u32[]{:S(2)}, u32[]{:S(2)}) %collective-permute-start.6) | collective-permute-done | bytes 524320 | tf_op jit(solution)/shard_map/ppermute | solution.py:20
  359.9 0.3 fusion.17
  360.5 0.6 fusion.2
  361.1 1.2 copy.115
  (31 shorter events, 2.0 us)
Async XLA Ops:
  0.0 9.8 %copy-start.2 = (f32[2]{0:T(128)S(1)}, f32[2]{0:T(128)}, u32[]{:S(2)}) copy-start(f32[2]{0:T(128)} %constant.62.clone) | copy-start | bytes 28
  148.5 43.5 %copy-start.3 = (f32[2]{0:T(128)S(1)}, f32[2]{0:T(128)}, u32[]{:S(2)}) copy-start(f32[2]{0:T(128)} %constant.65) | copy-start | bytes 28
  148.5 43.8 %copy-start = (f32[8,16,2,256]{3,1,2,0:T(8,128)S(1)}, f32[8,16,2,256]{3,1,2,0:T(8,128)}, u32[]{:S(2)}) copy-start(f32[8,16,2,256]{3,1,2,0:T(8,128)} %get-tuple-element.14) | copy-start | bytes 786436
  148.5 43.8 %copy-start.1 = (f32[8,16,2,256]{3,1,2,0:T(8,128)S(1)}, f32[8,16,2,256]{3,1,2,0:T(8,128)}, u32[]{:S(2)}) copy-start(f32[8,16,2,256]{3,1,2,0:T(8,128)} %get-tuple-element.16) | copy-start | bytes 786436
  151.3 15.9 %collective-permute-start.1 = (f32[8,2,16,2,256]{4,2,3,1,0:T(8,128)S(1)}, f32[8,2,16,2,256]{4,2,3,1,0:T(8,128)S(1)}, u32[]{:S(2)}, u32[]{:S(2)}) collective-permute-start(f32[8,2,16,2,256]{4,2,3,1,0:T(8,128)S(1)} %copy.101), channel_id=1, source_target_pairs={{32,0},{64,32},{96,64},{128,96},{160,128},{192,160},{224,192},{256... | collective-permute-start | bytes 1572872 | tf_op jit(solution)/shard_map/ppermute | solution.py:21
  156.2 17.3 %collective-permute-start = (f32[8,2,16,2,256]{4,2,3,1,0:T(8,128)S(1)}, f32[8,2,16,2,256]{4,2,3,1,0:T(8,128)S(1)}, u32[]{:S(2)}, u32[]{:S(2)}) collective-permute-start(f32[8,2,16,2,256]{4,2,3,1,0:T(8,128)S(1)} %copy.101), channel_id=1, source_target_pairs={{0,32},{32,64},{64,96},{96,128},{128,160},{160,192},{192,224},{224... | collective-permute-start | bytes 1572872 | tf_op jit(solution)/shard_map/ppermute | solution.py:20
  173.7 14.2 %collective-permute-start.3 = (f32[8,2,16,2,256]{4,2,3,1,0:T(8,128)S(1)}, f32[8,2,16,2,256]{4,2,3,1,0:T(8,128)S(1)}, u32[]{:S(2)}, u32[]{:S(2)}) collective-permute-start(f32[8,2,16,2,256]{4,2,3,1,0:T(8,128)S(1)} %get-tuple-element.7), channel_id=1, source_target_pairs={{32,0},{64,32},{96,64},{128,96},{160,128},{192,160},{224,192},{256... | collective-permute-start | bytes 1572872 | tf_op jit(solution)/shard_map/ppermute | solution.py:21
  175.6 16.3 %collective-permute-start.2 = (f32[8,2,16,2,256]{4,2,3,1,0:T(8,128)S(1)}, f32[8,2,16,2,256]{4,2,3,1,0:T(8,128)S(1)}, u32[]{:S(2)}, u32[]{:S(2)}) collective-permute-start(f32[8,2,16,2,256]{4,2,3,1,0:T(8,128)S(1)} %get-tuple-element.7), channel_id=1, source_target_pairs={{0,32},{32,64},{64,96},{96,128},{128,160},{160,192},{192,224},{224... | collective-permute-start | bytes 1572872 | tf_op jit(solution)/shard_map/ppermute | solution.py:20
  321.6 15.4 %collective-permute-start.5 = (f32[8,2,16,2,256]{4,2,3,1,0:T(8,128)S(1)}, f32[8,2,16,2,256]{4,2,3,1,0:T(8,128)S(1)}, u32[]{:S(2)}, u32[]{:S(2)}) collective-permute-start(f32[8,2,16,2,256]{4,2,3,1,0:T(8,128)S(1)} %copy.114), channel_id=1, source_target_pairs={{32,0},{64,32},{96,64},{128,96},{160,128},{192,160},{224,192},{256... | collective-permute-start | bytes 1572872 | tf_op jit(solution)/shard_map/ppermute | solution.py:21
  323.6 17.5 %collective-permute-start.4 = (f32[8,2,16,2,256]{4,2,3,1,0:T(8,128)S(1)}, f32[8,2,16,2,256]{4,2,3,1,0:T(8,128)S(1)}, u32[]{:S(2)}, u32[]{:S(2)}) collective-permute-start(f32[8,2,16,2,256]{4,2,3,1,0:T(8,128)S(1)} %copy.114), channel_id=1, source_target_pairs={{0,32},{32,64},{64,96},{96,128},{128,160},{160,192},{192,224},{224... | collective-permute-start | bytes 1572872 | tf_op jit(solution)/shard_map/ppermute | solution.py:20
  341.3 14.5 %collective-permute-start.7 = (f32[8,2,16,2,256]{4,2,3,1,0:T(8,128)S(1)}, f32[8,2,16,2,256]{4,2,3,1,0:T(8,128)S(1)}, u32[]{:S(2)}, u32[]{:S(2)}) collective-permute-start(f32[8,2,16,2,256]{4,2,3,1,0:T(8,128)S(1)} %get-tuple-element.5), channel_id=1, source_target_pairs={{32,0},{64,32},{96,64},{128,96},{160,128},{192,160},{224,192},{256... | collective-permute-start | bytes 1572872 | tf_op jit(solution)/shard_map/ppermute | solution.py:21
  343.3 16.7 %collective-permute-start.6 = (f32[8,2,16,2,256]{4,2,3,1,0:T(8,128)S(1)}, f32[8,2,16,2,256]{4,2,3,1,0:T(8,128)S(1)}, u32[]{:S(2)}, u32[]{:S(2)}) collective-permute-start(f32[8,2,16,2,256]{4,2,3,1,0:T(8,128)S(1)} %get-tuple-element.5), channel_id=1, source_target_pairs={{0,32},{32,64},{64,96},{96,128},{128,160},{160,192},{192,224},{224... | collective-permute-start | bytes 1572872 | tf_op jit(solution)/shard_map/ppermute | solution.py:20
where the time goes:
time: 369 us; the launch traced here: 363 us
  blocking collectives  161 us (44%)
  local copies, waits for them, and re-layouts  101 us (27%)
  waiting for transfers between devices  54.1 us (15%)
  starting transfers between devices  24.3 us (7%)
  other arithmetic  14.5 us (4%)
  matrix products  6.96 us (2%)
    all_to_all x2, blocking collectives, regroup_columns(): lax.all_to_all(current, 'pencil', split_axis=4, concat_axis=0, tiled=True)  86.8 us
    all_to_all x2, blocking collectives, regroup_rows(): lax.all_to_all(current, 'pencil', split_axis=0, concat_axis=4, tiled=True)  74.5 us
    unnamed x17, local copies, waits for them, and re-layouts  42.1 us
    ppermute x4, waiting for transfers between devices, extended(): after = lax.ppermute(initial, axis, down)  35.7 us
    all_to_all x7, local copies, waits for them, and re-layouts, regroup_columns(): lax.all_to_all(current, 'pencil', split_axis=4, concat_axis=0, tiled=True)  22.3 us
    ppermute x4, waiting for transfers between devices, extended(): before = lax.ppermute(last, axis, up)  18.3 us
    all_to_all x4, local copies, waits for them, and re-layouts, regroup_rows(): lax.all_to_all(current, 'pencil', split_axis=0, concat_axis=4, tiled=True)  15 us
    ppermute x4, starting transfers between devices, extended(): before = lax.ppermute(last, axis, up)  13.7 us
  transfers between devices with their start and end apart: 8, of which 8 were waited for; matrix products, arithmetic and copies ran while one was open for 0% of the time, Pallas kernels for 0%

commit v1 on v0

v1 whole, which is shorter than its diff:
```python
import jax
import jax.numpy as jnp
from jax import lax
from jax.experimental import pallas as pl
from jax.experimental.pallas import tpu as pltpu
from jax.sharding import PartitionSpec as P


MESH = pl.DeviceIdType.MESH
F32 = jnp.float32
BF16 = jnp.bfloat16
STEP = 0.1
GRID = 0.5
CHARGE = 3.0
BAND = 0.3
NP = 32
NS = 16
L2 = 8
L3 = 2
C = 16
N = 256
CHUNKS = 2


def iota(shape, dim):
    return lax.broadcasted_iota(jnp.int32, shape, dim)


def split2(x):
    high = x.astype(BF16)
    return high, (x - high.astype(F32)).astype(BF16)


def split3(x):
    high = x.astype(BF16)
    rest = x - high.astype(F32)
    middle = rest.astype(BF16)
    return high, middle, (rest - middle.astype(F32)).astype(BF16)


def product(a, b, contract=((1,), (0,))):
    def one(x, y):
        return lax.dot_general(x, y, (contract, ((), ())), preferred_element_type=F32)

    return one(a[0], b[0]) + (one(a[0], b[1]) + one(a[1], b[0]))


def column(row, count):
    shape = (count, row.shape[1])
    return jnp.sum(jnp.where(iota(shape, 0) == iota(shape, 1), row, jnp.zeros_like(row)), axis=1, keepdims=True)


def radial(position, weight):
    radius = GRID * (position.astype(F32) + 1.0)
    return -CHARGE / radius + weight / (radius * radius)


def flip_blocks(x):
    row, group = iota((1, 8, 128), 1), iota((1, 8, 128), 2) // 16
    for bit in (4, 2, 1):
        lanes = 16 * bit
        has_row, has_group = (row // bit) % 2, (group // bit) % 2
        down = pltpu.roll(pltpu.roll(x, bit, 1), 128 - lanes, 2)
        if bit == 4:
            up = down
        else:
            up = pltpu.roll(pltpu.roll(x, 8 - bit, 1), lanes, 2)
        x = jnp.where(has_row == has_group, x, jnp.where(has_row == 1, down, up))
    return x


def band(x):
    zero = jnp.zeros((2,) + x.shape[1:], F32)
    padded = jnp.concatenate([zero, x, zero], axis=0)
    n = x.shape[0]
    outer = padded[0:n] + padded[4 : n + 4]
    inner = padded[1 : n + 1] + padded[3 : n + 3]
    return (BAND / 24.0) * (outer - 16.0 * inner + 30.0 * x)


def body(
    x_ref,
    prop_ref,
    len_ref,
    cent_ref,
    pair_ref,
    str_ref,
    o_ref,
    cos_a,
    sin_a,
    wl_a,
    lv_a,
    kron_hi,
    kron_lo,
    mix_hi,
    mix_lo,
    w1_hi,
    w1_lo,
    q2_hi,
    q2_lo,
    wf_hi,
    wf_lo,
    cos_d,
    sin_d,
    u_hi,
    u_lo,
    len_col,
    len_in,
    len_out,
    ybuf,
    bbuf,
    sbuf,
    dbuf,
    ebuf,
    hbuf,
    gbuf,
    rbuf,
    send_sem,
    recv_sem,
    len_send,
    len_recv,
):
    p = lax.axis_index("pencil")
    s = lax.axis_index("slab")
    barrier = pltpu.get_barrier_semaphore()

    def far(n, size):
        half = (n + 1) // 2
        return size // 2 + (1 - 2 * (n % 2)) * half

    def pencil_peer(n):
        return lax.rem(p + far(n, NP), NP)

    def slab_peer(n):
        return lax.rem(s + far(n, NS), NS)

    @pl.loop(0, NP - 1)
    def _(n):
        pl.semaphore_signal(barrier, inc=1, device_id=(s, pencil_peer(n)), device_id_type=MESH)

    @pl.loop(0, NS - 1)
    def _(n):
        pl.semaphore_signal(barrier, inc=1, device_id=(slab_peer(n), p), device_id_type=MESH)

    def copy(src, dst, k, device):
        return pltpu.make_async_remote_copy(
            src_ref=src,
            dst_ref=dst,
            send_sem=send_sem.at[k],
            recv_sem=recv_sem.at[k],
            device_id=device,
            device_id_type=MESH,
        )

    def pencil_exchange(src, dst, chunk, k):
        @pl.loop(0, NP - 1)
        def _(n):
            q = pencil_peer(n)
            copy(src.at[chunk, q], dst.at[chunk, p], k, (s, q)).start()

        dst[chunk, pl.ds(p, 1)] = src[chunk, pl.ds(p, 1)]

    def slab_exchange(src, dst, chunk, k):
        @pl.loop(0, NS - 1)
        def _(n):
            q = slab_peer(n)
            copy(src.at[chunk, q], dst.at[chunk, s], k, (q, p)).start()

        dst[chunk, pl.ds(s, 1)] = src[chunk, pl.ds(s, 1)]

    def arrived(buf, chunk, k, count):
        part = buf.at[chunk, pl.ds(0, count - 1)]
        copy(part, part, k, (s, p)).wait_recv()

    def left(buf, chunk, k, count):
        part = buf.at[chunk, pl.ds(0, count - 1)]
        copy(part, part, k, (s, p)).wait_send()

    lens = len_ref[...].astype(F32)
    lane = iota((8, 128), 1)
    len_tile = jnp.zeros((8, 128), F32)
    len_rows = []
    for i3 in range(L3):
        col = column(lens[i3 : i3 + 1], L2)
        len_rows.append(col)
        len_tile = len_tile + jnp.where(lane == L3 * s + i3, col, jnp.zeros_like(col))
    len_out[0] = len_tile
    len_a = jnp.concatenate(len_rows, axis=0)

    strength = str_ref[...]
    first, second = pair_ref[0:1, :], pair_ref[1:2, :]

    def hot_rows(labels):
        return (iota((N, 32), 0) % C == labels).astype(F32)

    def hot_cols(labels):
        shape = (32, 32)
        col = jnp.sum(jnp.where(iota(shape, 0) == iota(shape, 1), labels, 0), axis=1, keepdims=True)
        return (iota((32, N), 1) % C == col).astype(F32)

    rows_1, rows_2, cols_1, cols_2 = hot_rows(first), hot_rows(second), hot_cols(first), hot_cols(second)
    tiled = jnp.zeros((N, N), F32)
    for part in split3(strength):
        scale = part.astype(F32)
        tiled = tiled + jnp.dot((rows_1 * scale).astype(BF16), cols_2.astype(BF16), preferred_element_type=F32)
        tiled = tiled + jnp.dot((rows_2 * scale).astype(BF16), cols_1.astype(BF16), preferred_element_type=F32)
    row, col = iota((N, N), 0), iota((N, N), 1)
    kron_hi[...], kron_lo[...] = split2(jnp.where(row // C == col // C, tiled, 0.0))
    row, col = iota((128, 128), 0), iota((128, 128), 1)
    same = (row // C) % 4 == (col // C) % 4
    sign = (row // 64 - col // 64).astype(F32)
    mix_hi[...], mix_lo[...] = split2(jnp.where(same, tiled[:128, :128] * sign, 0.0))

    half = 0.5 * STEP
    cent = cent_ref[...]
    cent_col = [column(cent[e : e + 1], C) for e in range(3)]
    angle_1 = half * radial(iota((C, N), 1), cent_col[0])
    cos_1, sin_1 = jnp.cos(angle_1), jnp.sin(angle_1)
    lane = iota((C, 16), 1)
    angle_23 = half * (radial(L2 * p + lane % L2, cent_col[1]) + radial(L3 * s + lane // L2, cent_col[2]))
    cos_23, sin_23 = jnp.cos(angle_23), jnp.sin(angle_23)
    for m in range(16):
        c23, s23 = cos_23[:, m : m + 1], sin_23[:, m : m + 1]
        cos_a[m * C : (m + 1) * C] = cos_1 * c23 - sin_1 * s23
        sin_a[m * C : (m + 1) * C] = sin_1 * c23 + cos_1 * s23
    row, col = iota((16, N), 0), iota((16, N), 1)
    farthest = jnp.maximum(jnp.maximum(L2 * p + row % L2, L3 * s + row // L2), col).astype(F32)
    live = (col.astype(F32) < len_a).astype(F32)
    lv_a[...] = live
    wl_a[...] = live * (half / (1.0 + 0.02 * farthest))

    sub = iota((1, 8, 2 * N), 1)

    def interleaved(re, im):
        top = jnp.concatenate([re, -im], axis=1).reshape(NP, 8, 2 * N)
        low = jnp.concatenate([im, re], axis=1).reshape(NP, 8, 2 * N)
        early = jnp.where(sub < 4, top, pltpu.roll(low, 4, 1))
        late = jnp.where(sub < 4, pltpu.roll(top, 4, 1), low)
        return [split2(v.reshape(N, 2 * N)) for v in (early, late)]

    for chunk, (high, low) in enumerate(interleaved(prop_ref[0], prop_ref[1])):
        w1_hi[chunk], w1_lo[chunk] = high, low

    kron = (kron_hi[...], kron_lo[...])

    def potential(re, im):
        cosine, sine = cos_a[...], sin_a[...]
        turned_re = re * cosine + im * sine
        turned_im = im * cosine - re * sine
        mixed_re = product(kron, split2(turned_im))
        mixed_im = product(kron, split2(turned_re))

        def rows(a):
            return jnp.concatenate([jnp.broadcast_to(a[m : m + 1], (C, N)) for m in range(16)], axis=0)

        weight, alive = rows(wl_a[...]), rows(lv_a[...])
        return turned_re * alive + weight * mixed_re, turned_im * alive - weight * mixed_im

    def load(part):
        blocks = []
        for i3 in range(L3):
            for i2 in range(L2):
                base = (i2 * 2 + part) * 64 + i3
                blocks.append(
                    jnp.concatenate([x_ref[pl.ds(base + 2 * l, C, stride=4), :] for l in range(2)], axis=1)
                )
        return jnp.concatenate(blocks, axis=0)

    v_re, v_im = potential(load(0), load(1))
    u_hi[...], u_lo[...] = split2(jnp.concatenate([v_re, v_im], axis=1))
    u = (u_hi[...], u_lo[...])

    for chunk in range(CHUNKS):
        y = product((w1_hi[chunk], w1_lo[chunk]), u, ((1,), (1,)))
        for i3 in range(L3):
            ybuf[chunk, :, i3] = y[:, i3 * 128 : (i3 + 1) * 128].reshape(NP, 8, 128)
        if chunk == 0:
            pl.semaphore_wait(barrier, NP + NS - 2)
        pencil_exchange(ybuf, bbuf, chunk, chunk)

    root = s == p // 2

    def len_copy(src, dst, k, device):
        return pltpu.make_async_remote_copy(
            src_ref=src,
            dst_ref=dst,
            send_sem=len_send.at[k],
            recv_sem=len_recv.at[k],
            device_id=device,
            device_id_type=MESH,
        )

    @pl.when(jnp.logical_not(root))
    def _():
        first_copy = len_copy(len_out.at[0], len_col.at[s], 0, (p // 2, p))
        first_copy.start()
        first_copy.wait_send()

    @pl.when(root)
    def _():
        len_col[pl.ds(s, 1)] = len_out[pl.ds(0, 1)]
        part = len_col.at[pl.ds(0, NS - 1)]
        len_copy(part, part, 0, (s, p)).wait_recv()
        total = jnp.sum(len_col[...], axis=0)
        len_out[1] = total
        len_in[pl.ds(lax.rem(p, 2), 1)] = total[None]

        @pl.loop(0, NP - 1)
        def _(n):
            len_copy(len_out.at[1], len_in.at[lax.rem(p, 2)], 1, (s, pencil_peer(n))).start()

        @pl.loop(0, NP - 1)
        def _(n):
            len_copy(len_out.at[1], len_in.at[0], 1, (s, p)).wait_send()

        len_copy(len_in.at[0], len_in.at[0], 1, (s, p)).wait_recv()

    @pl.when(jnp.logical_not(root))
    def _():
        len_copy(len_in, len_in, 1, (s, p)).wait_recv()

    re, im = prop_ref[0], prop_ref[1]
    q2_hi[...], q2_lo[...] = split2(jnp.concatenate([re, im], axis=0))
    for chunk, (high, low) in enumerate(interleaved(re.T, -im.T)):
        wf_hi[chunk], wf_lo[chunk] = high, low

    lane = iota((C, 128), 1)
    cent_row = [
        jnp.sum(jnp.where(iota((C, 128), 0) == lane % C, col, 0.0), axis=0, keepdims=True) for col in cent_col
    ]
    lane = iota((1, 128), 1)
    rows_2 = C * s + iota((16, 128), 0)
    angle_2 = STEP * radial(rows_2, cent_row[1])
    angle_3 = STEP * radial(iota((32, 128), 0), cent_row[2])
    cos_3, sin_3 = jnp.cos(angle_3), jnp.sin(angle_3)
    turn = jnp.where(lane < 64, 1.0, -1.0)
    for chunk in range(CHUNKS):
        angle_12 = angle_2 + STEP * radial(8 * p + 4 * chunk + (lane // C) % 4, cent_row[0])
        cos_12, sin_12 = jnp.cos(angle_12), jnp.sin(angle_12)
        for i3 in range(32):
            c3, s3 = cos_3[i3 : i3 + 1], sin_3[i3 : i3 + 1]
            cos_d[chunk, i3] = cos_12 * c3 - sin_12 * s3
            sin_d[chunk, i3] = turn * (sin_12 * c3 + cos_12 * s3)

    q2 = (q2_hi[...], q2_lo[...])

    def second_line(z):
        both = product(q2, split2(z))
        a, b = both[:N], both[N:]
        lane = iota((1, 128), 1)
        sign = jnp.where(lane < 64, -1.0, 1.0)
        return [
            a[:, i * 128 : (i + 1) * 128] + sign * pltpu.roll(b[:, i * 128 : (i + 1) * 128], 64, 1) for i in range(L3)
        ]

    def third_line(psi):
        g1 = band(psi)
        g2 = band(g1)
        return psi + turn * pltpu.roll(g1, 64, 2) - 0.5 * g2

    def third_potential(psi, chunk):
        turned = psi * cos_d[chunk] + sin_d[chunk] * pltpu.roll(psi, 64, 2)
        mixed = product(split2(turned.reshape(512, 128)), (mix_hi[...], mix_lo[...])).reshape(32, 16, 128)
        first_pos = 8 * p + 4 * chunk + (lane // C) % 4
        both = jnp.maximum(rows_2, first_pos)
        lengths = jnp.concatenate([len_in[0], len_in[1]], axis=0)
        out = []
        for i3 in range(32):
            weight = STEP / (1.0 + 0.02 * jnp.maximum(both, i3).astype(F32))
            alive = first_pos.astype(F32) < lengths[:, i3 : i3 + 1]
            out.append(jnp.where(alive, turned[i3] + weight * mixed[i3], 0.0))
        return jnp.stack(out, axis=0)

    for chunk in range(CHUNKS):
        arrived(bbuf, chunk, chunk, NP)
        z = [flip_blocks(bbuf[chunk, :, i3]).reshape(N, 128) for i3 in range(L3)]
        z = second_line(jnp.concatenate(z, axis=1))
        for i3 in range(L3):
            sbuf[chunk, :, i3] = z[i3].reshape(NS, 16, 128)
        slab_exchange(sbuf, dbuf, chunk, 2 + chunk)

        arrived(dbuf, chunk, 2 + chunk, NS)
        psi = third_line(dbuf[chunk].reshape(32, 16, 128))
        psi = third_line(third_potential(psi, chunk))
        ebuf[chunk] = psi.reshape(NS, L3, 16, 128)
        slab_exchange(ebuf, hbuf, chunk, 4 + chunk)

        arrived(hbuf, chunk, 4 + chunk, NS)
        z = [hbuf[chunk, :, i3].reshape(N, 128) for i3 in range(L3)]
        z = second_line(jnp.concatenate(z, axis=1))
        for i3 in range(L3):
            gbuf[chunk, :, i3] = flip_blocks(z[i3].reshape(NP, 8, 128))
        pencil_exchange(gbuf, rbuf, chunk, 6 + chunk)

    out = jnp.zeros((N, 2 * N), F32)
    for chunk in range(CHUNKS):
        arrived(rbuf, chunk, 6 + chunk, NP)
        r = jnp.concatenate([rbuf[chunk, :, i3].reshape(N, 128) for i3 in range(L3)], axis=1)
        out = out + product(split2(r.T), (wf_hi[chunk], wf_lo[chunk]))

    out = potential(out[:, :N], out[:, N:])
    for part in range(2):
        for i3 in range(L3):
            for i2 in range(L2):
                base = (i2 * 2 + part) * 64 + i3
                start = (i3 * L2 + i2) * C
                for l in range(2):
                    o_ref[pl.ds(base + 2 * l, C, stride=4), :] = out[part][start : start + C, l * 128 : (l + 1) * 128]

    for chunk in range(CHUNKS):
        left(ybuf, chunk, chunk, NP)
        left(sbuf, chunk, 2 + chunk, NS)
        left(ebuf, chunk, 4 + chunk, NS)
        left(gbuf, chunk, 6 + chunk, NP)


def on_device(wavefunction, propagator, lengths, centrifugal, channel_pairs, strengths):
    shape = wavefunction.shape
    x = wavefunction.reshape(8, 2, 16, 2, 2, 128).transpose(0, 1, 2, 4, 3, 5).reshape(1024, 128)

    def vmem(*dims, dtype=F32):
        return pltpu.VMEM(dims, dtype)

    scratch = [
        vmem(N, N),
        vmem(N, N),
        vmem(16, N),
        vmem(16, N),
        vmem(N, N, dtype=BF16),
        vmem(N, N, dtype=BF16),
        vmem(128, 128, dtype=BF16),
        vmem(128, 128, dtype=BF16),
        vmem(CHUNKS, N, 2 * N, dtype=BF16),
        vmem(CHUNKS, N, 2 * N, dtype=BF16),
        vmem(2 * N, N, dtype=BF16),
        vmem(2 * N, N, dtype=BF16),
        vmem(CHUNKS, N, 2 * N, dtype=BF16),
        vmem(CHUNKS, N, 2 * N, dtype=BF16),
        vmem(CHUNKS, 32, 16, 128),
        vmem(CHUNKS, 32, 16, 128),
        vmem(N, 2 * N, dtype=BF16),
        vmem(N, 2 * N, dtype=BF16),
        vmem(NS, 8, 128),
        vmem(2, 8, 128),
        vmem(2, 8, 128),
        vmem(CHUNKS, NP, L3, 8, 128),
        vmem(CHUNKS, NP, L3, 8, 128),
        vmem(CHUNKS, NS, L3, 16, 128),
        vmem(CHUNKS, NS, L3, 16, 128),
        vmem(CHUNKS, NS, L3, 16, 128),
        vmem(CHUNKS, NS, L3, 16, 128),
        vmem(CHUNKS, NP, L3, 8, 128),
        vmem(CHUNKS, NP, L3, 8, 128),
        pltpu.SemaphoreType.DMA((8,)),
        pltpu.SemaphoreType.DMA((8,)),
        pltpu.SemaphoreType.DMA((2,)),
        pltpu.SemaphoreType.DMA((2,)),
    ]
    whole = pl.BlockSpec(memory_space=pltpu.VMEM)
    out = pl.pallas_call(
        body,
        out_shape=jax.ShapeDtypeStruct((1024, 128), F32),
        in_specs=[whole] * 6,
        out_specs=whole,
        scratch_shapes=scratch,
        compiler_params=pltpu.CompilerParams(
            collective_id=0, has_side_effects=True, vmem_limit_bytes=48 * 2**20
        ),
        name="propagate",
    )(x, propagator, lengths, centrifugal, channel_pairs.T, strengths.reshape(1, 32))
    return out.reshape(8, 2, 16, 2, 2, 128).transpose(0, 1, 2, 4, 3, 5).reshape(shape)


def solution(mesh):
    in_specs = (P("pencil", None, None, "slab", None), P(), P("slab", "pencil"), P(), P(), P())
    out_specs = P("pencil", None, None, "slab", None)
    return jax.shard_map(
        on_device, mesh=mesh, in_specs=in_specs, out_specs=out_specs, check_vma=False
    )
```

time: 369 us -> 91.1 us (0.25)
  the two profiles are of different devices: /device:TPU:24 before, /device:TPU:1 now
where the time goes in v1:
time: 91.1 us; the launch traced here: 90.8 us
  Pallas kernels  87.2 us (96%)
  local copies, waits for them, and re-layouts  3.58 us (4%)
    pallas_call x1, Pallas kernels, on_device(): pl.pallas_call(body, out_shape=jax.ShapeDtypeStruct((1024, 128), F32), in...  87.2 us
    unnamed x13, local copies, waits for them, and re-layouts  3.58 us

profile of v1, /device:TPU:1, one launch (start us, length us, event | category | flops | bytes accessed | tf_op | source)
XLA Modules:
  0.0 90.8 jit_solution(8775465159611379807)
XLA Ops:
  0.0 0.0 copy-start.4
  0.0 0.0 copy-start.2
  0.0 0.0 copy-start.3
  0.0 0.0 copy-start.5
  0.0 0.7 copy-done.4
  0.7 0.0 copy-done.2
  0.7 0.0 copy-done.3
  0.7 0.0 copy-done.5
  0.7 0.0 copy-start
  0.7 1.0 %copy-done = f32[8,2,16,2,256]{4,3,2,1,0:T(2,128)S(1)} copy-done((f32[8,2,16,2,256]{4,3,2,1,0:T(2,128)S(1)}, f32[8,2,16,2,256]{4,3,2,1,0:T(2,128)}, u32[]{:S(2)}) %copy-start) | copy-done | bytes 524312
  1.8 0.0 copy-start.1
  1.8 1.0 %copy-done.1 = f32[2,256,256]{2,1,0:T(8,128)S(1)} copy-done((f32[2,256,256]{2,1,0:T(8,128)S(1)}, f32[2,256,256]{2,1,0:T(8,128)}, u32[]{:S(2)}) %copy-start.1) | copy-done | bytes 524312
  2.8 87.2 %propagate.1 = f32[1024,128]{1,0:T(8,128)S(1)} custom-call(f32[1024,128]{1,0:T(8,128)S(1)} %bitcast.13, f32[2,256,256]{2,1,0:T(8,128)S(1)} %copy-done.1, s32[2,8]{1,0:T(2,128)S(1)} %copy-done.3, f32[3,16]{1,0:T(4,128)S(1)} %copy-done.2, s32[2,32]{1,0:T(2,128)S(1)} %bitcast.14, f32[1,32]{1,0:T(1,128)S(1)} %bitcast.15), custom_call_target="tpu_custom_call" | custom-call | tf_op jit(solution)/shard_map/propagate/pallas_call | solution.py:460
  90.0 0.8 copy.10
Async XLA Ops:
  0.0 0.7 copy-start.4
  0.0 0.7 copy-start.2
  0.0 0.7 copy-start.3
  0.0 0.7 copy-start.5
  0.7 1.0 %copy-start = (f32[8,2,16,2,256]{4,3,2,1,0:T(2,128)S(1)}, f32[8,2,16,2,256]{4,3,2,1,0:T(2,128)}, u32[]{:S(2)}) copy-start(f32[8,2,16,2,256]{4,3,2,1,0:T(2,128)} %param.6) | copy-start | bytes 1572868
  1.8 1.0 %copy-start.1 = (f32[2,256,256]{2,1,0:T(8,128)S(1)}, f32[2,256,256]{2,1,0:T(8,128)}, u32[]{:S(2)}) copy-start(f32[2,256,256]{2,1,0:T(8,128)} %prop_ref.1) | copy-start | bytes 1572868

commit v2 on v1

--- a/solution.py
+++ b/solution.py
@@ -19,7 +19,7 @@
 L3 = 2
 C = 16
 N = 256
-CHUNKS = 2
+CHUNKS = 4
 
 
 def iota(shape, dim):
@@ -70,22 +70,34 @@
 
 
 def band(x):
-    zero = jnp.zeros((2,) + x.shape[1:], F32)
-    padded = jnp.concatenate([zero, x, zero], axis=0)
-    n = x.shape[0]
-    outer = padded[0:n] + padded[4 : n + 4]
-    inner = padded[1 : n + 1] + padded[3 : n + 3]
-    return (BAND / 24.0) * (outer - 16.0 * inner + 30.0 * x)
+    low = (iota((1, 1, 128), 2) // 32) % 2 == 0
+    swapped = jnp.where(low, pltpu.roll(x, 96, 2), pltpu.roll(x, 32, 2))
+    zero = jnp.zeros((1,) + x.shape[1:], F32)
+
+    def before(a):
+        return jnp.concatenate([zero, a[:-1]], axis=0)
+
+    def after(a):
+        return jnp.concatenate([a[1:], zero], axis=0)
+
+    inner = swapped + jnp.where(low, before(swapped), after(swapped))
+    return (BAND / 24.0) * (before(x) + after(x) - 16.0 * inner + 30.0 * x)
 
 
 def body(
+    x_hbm,
+    prop_hbm,
+    len_hbm,
+    cent_hbm,
+    pair_hbm,
+    str_hbm,
+    o_ref,
     x_ref,
     prop_ref,
     len_ref,
     cent_ref,
     pair_ref,
     str_ref,
-    o_ref,
     cos_a,
     sin_a,
     wl_a,
@@ -115,6 +127,7 @@
     hbuf,
     gbuf,
     rbuf,
+    in_sem,
     send_sem,
     recv_sem,
     len_send,
@@ -141,6 +154,18 @@
     @pl.loop(0, NS - 1)
     def _(n):
         pl.semaphore_signal(barrier, inc=1, device_id=(slab_peer(n), p), device_id_type=MESH)
+
+    pairs = [
+        (pair_hbm, pair_ref),
+        (str_hbm, str_ref),
+        (cent_hbm, cent_ref),
+        (len_hbm, len_ref),
+        (x_hbm, x_ref),
+        (prop_hbm, prop_ref),
+    ]
+    inputs = [pltpu.make_async_copy(src, dst, in_sem.at[i]) for i, (src, dst) in enumerate(pairs)]
+    for item in inputs:
+        item.start()
 
     def copy(src, dst, k, device):
         return pltpu.make_async_remote_copy(
@@ -176,17 +201,8 @@
         part = buf.at[chunk, pl.ds(0, count - 1)]
         copy(part, part, k, (s, p)).wait_send()
 
-    lens = len_ref[...].astype(F32)
-    lane = iota((8, 128), 1)
-    len_tile = jnp.zeros((8, 128), F32)
-    len_rows = []
-    for i3 in range(L3):
-        col = column(lens[i3 : i3 + 1], L2)
-        len_rows.append(col)
-        len_tile = len_tile + jnp.where(lane == L3 * s + i3, col, jnp.zeros_like(col))
-    len_out[0] = len_tile
-    len_a = jnp.concatenate(len_rows, axis=0)
-
+    inputs[0].wait()
+    inputs[1].wait()
     strength = str_ref[...]
     first, second = pair_ref[0:1, :], pair_ref[1:2, :]
 
@@ -211,6 +227,8 @@
     sign = (row // 64 - col // 64).astype(F32)
     mix_hi[...], mix_lo[...] = split2(jnp.where(same, tiled[:128, :128] * sign, 0.0))
 
+    inputs[2].wait()
+    inputs[3].wait()
     half = 0.5 * STEP
     cent = cent_ref[...]
     cent_col = [column(cent[e : e + 1], C) for e in range(3)]
@@ -223,24 +241,25 @@
         c23, s23 = cos_23[:, m : m + 1], sin_23[:, m : m + 1]
         cos_a[m * C : (m + 1) * C] = cos_1 * c23 - sin_1 * s23
         sin_a[m * C : (m + 1) * C] = sin_1 * c23 + cos_1 * s23
+
+    lens = len_ref[...].astype(F32)
+    lane = iota((8, 128), 1)
+    len_tile = jnp.zeros((8, 128), F32)
+    len_rows = []
+    for i3 in range(L3):
+        col = column(lens[i3 : i3 + 1], L2)
+        len_rows.append(col)
+        len_tile = len_tile + jnp.where(lane == L3 * s + i3, col, jnp.zeros_like(col))
+    len_out[0] = len_tile
+    len_a = jnp.concatenate(len_rows, axis=0)
+
     row, col = iota((16, N), 0), iota((16, N), 1)
     farthest = jnp.maximum(jnp.maximum(L2 * p + row % L2, L3 * s + row // L2), col).astype(F32)
     live = (col.astype(F32) < len_a).astype(F32)
     lv_a[...] = live
     wl_a[...] = live * (half / (1.0 + 0.02 * farthest))
 
-    sub = iota((1, 8, 2 * N), 1)
-
-    def interleaved(re, im):
-        top = jnp.concatenate([re, -im], axis=1).reshape(NP, 8, 2 * N)
-        low = jnp.concatenate([im, re], axis=1).reshape(NP, 8, 2 * N)
-        early = jnp.where(sub < 4, top, pltpu.roll(low, 4, 1))
-        late = jnp.where(sub < 4, pltpu.roll(top, 4, 1), low)
-        return [split2(v.reshape(N, 2 * N)) for v in (early, late)]
-
-    for chunk, (high, low) in enumerate(interleaved(prop_ref[0], prop_ref[1])):
-        w1_hi[chunk], w1_lo[chunk] = high, low
-
+    inputs[4].wait()
     kron = (kron_hi[...], kron_lo[...])
 
     def potential(re, im):
@@ -270,13 +289,28 @@
     u_hi[...], u_lo[...] = split2(jnp.concatenate([v_re, v_im], axis=1))
     u = (u_hi[...], u_lo[...])
 
-    for chunk in range(CHUNKS):
-        y = product((w1_hi[chunk], w1_lo[chunk]), u, ((1,), (1,)))
-        for i3 in range(L3):
-            ybuf[chunk, :, i3] = y[:, i3 * 128 : (i3 + 1) * 128].reshape(NP, 8, 128)
-        if chunk == 0:
-            pl.semaphore_wait(barrier, NP + NS - 2)
-        pencil_exchange(ybuf, bbuf, chunk, chunk)
+    inputs[5].wait()
+    sub = iota((1, 8, 2 * N), 1)
+
+    def interleaved(re, im):
+        top = jnp.concatenate([re, -im], axis=1).reshape(NP, 8, 2 * N)
+        low = jnp.concatenate([im, re], axis=1).reshape(NP, 8, 2 * N)
+        early = jnp.where(sub < 4, top, pltpu.roll(low, 4, 1))
+        late = jnp.where(sub < 4, pltpu.roll(top, 4, 1), low)
+        return [split2(v.reshape(N, 2 * N)) for v in (early, late)]
+
+    for part, (high, low) in enumerate(interleaved(prop_ref[0], prop_ref[1])):
+        w1_hi[part], w1_lo[part] = high, low
+
+    outer = (iota((1, 8, 128), 1) // 2) % 2 == 0
+
+    def first_line(half_of):
+        y = product((w1_hi[half_of], w1_lo[half_of]), u, ((1,), (1,)))
+        y = [y[:, i * 128 : (i + 1) * 128].reshape(NP, 8, 128) for i in range(L3)]
+        ybuf[2 * half_of] = jnp.where(outer, y[0], pltpu.roll(y[1], 2, 1))
+        ybuf[2 * half_of + 1] = jnp.where(outer, pltpu.roll(y[0], 6, 1), y[1])
+
+    first_line(0)
 
     root = s == p // 2
 
@@ -290,11 +324,14 @@
             device_id_type=MESH,
         )
 
+    pl.semaphore_wait(barrier, NP + NS - 2)
+
     @pl.when(jnp.logical_not(root))
     def _():
-        first_copy = len_copy(len_out.at[0], len_col.at[s], 0, (p // 2, p))
-        first_copy.start()
-        first_copy.wait_send()
+        len_copy(len_out.at[0], len_col.at[s], 0, (p // 2, p)).start()
+
+    pencil_exchange(ybuf, bbuf, 0, 0)
+    first_line(1)
 
     @pl.when(root)
     def _():
@@ -309,49 +346,42 @@
         def _(n):
             len_copy(len_out.at[1], len_in.at[lax.rem(p, 2)], 1, (s, pencil_peer(n))).start()
 
-        @pl.loop(0, NP - 1)
-        def _(n):
-            len_copy(len_out.at[1], len_in.at[0], 1, (s, p)).wait_send()
-
-        len_copy(len_in.at[0], len_in.at[0], 1, (s, p)).wait_recv()
-
-    @pl.when(jnp.logical_not(root))
-    def _():
-        len_copy(len_in, len_in, 1, (s, p)).wait_recv()
+    for chunk in range(1, CHUNKS):
+        pencil_exchange(ybuf, bbuf, chunk, chunk)
 
     re, im = prop_ref[0], prop_ref[1]
     q2_hi[...], q2_lo[...] = split2(jnp.concatenate([re, im], axis=0))
-    for chunk, (high, low) in enumerate(interleaved(re.T, -im.T)):
-        wf_hi[chunk], wf_lo[chunk] = high, low
+    for part, (high, low) in enumerate(interleaved(re.T, -im.T)):
+        wf_hi[part], wf_lo[part] = high, low
 
     lane = iota((C, 128), 1)
     cent_row = [
         jnp.sum(jnp.where(iota((C, 128), 0) == lane % C, col, 0.0), axis=0, keepdims=True) for col in cent_col
     ]
     lane = iota((1, 128), 1)
-    rows_2 = C * s + iota((16, 128), 0)
-    angle_2 = STEP * radial(rows_2, cent_row[1])
-    angle_3 = STEP * radial(iota((32, 128), 0), cent_row[2])
+    second_pos = 16 * s + iota((16, 128), 0)
+    third_pos = L3 * iota((NS, 128), 0) + (lane // 32) % 2
+
+    def first_pos(chunk):
+        return 8 * p + 2 * chunk + (lane // C) % 2
+
+    angle_2 = STEP * radial(second_pos, cent_row[1])
+    angle_3 = STEP * radial(third_pos, cent_row[2])
     cos_3, sin_3 = jnp.cos(angle_3), jnp.sin(angle_3)
     turn = jnp.where(lane < 64, 1.0, -1.0)
     for chunk in range(CHUNKS):
-        angle_12 = angle_2 + STEP * radial(8 * p + 4 * chunk + (lane // C) % 4, cent_row[0])
+        angle_12 = angle_2 + STEP * radial(first_pos(chunk), cent_row[0])
         cos_12, sin_12 = jnp.cos(angle_12), jnp.sin(angle_12)
-        for i3 in range(32):
-            c3, s3 = cos_3[i3 : i3 + 1], sin_3[i3 : i3 + 1]
-            cos_d[chunk, i3] = cos_12 * c3 - sin_12 * s3
-            sin_d[chunk, i3] = turn * (sin_12 * c3 + cos_12 * s3)
+        for i in range(NS):
+            c3, s3 = cos_3[i : i + 1], sin_3[i : i + 1]
+            cos_d[chunk, i] = cos_12 * c3 - sin_12 * s3
+            sin_d[chunk, i] = turn * (sin_12 * c3 + cos_12 * s3)
 
     q2 = (q2_hi[...], q2_lo[...])
 
     def second_line(z):
         both = product(q2, split2(z))
-        a, b = both[:N], both[N:]
-        lane = iota((1, 128), 1)
-        sign = jnp.where(lane < 64, -1.0, 1.0)
-        return [
-            a[:, i * 128 : (i + 1) * 128] + sign * pltpu.roll(b[:, i * 128 : (i + 1) * 128], 64, 1) for i in range(L3)
-        ]
+        return both[:N] - turn * pltpu.roll(both[N:], 64, 1)
 
     def third_line(psi):
         g1 = band(psi)
@@ -360,43 +390,61 @@
 
     def third_potential(psi, chunk):
         turned = psi * cos_d[chunk] + sin_d[chunk] * pltpu.roll(psi, 64, 2)
-        mixed = product(split2(turned.reshape(512, 128)), (mix_hi[...], mix_lo[...])).reshape(32, 16, 128)
-        first_pos = 8 * p + 4 * chunk + (lane // C) % 4
-        both = jnp.maximum(rows_2, first_pos)
+        mixed = product(split2(turned.reshape(N, 128)), (mix_hi[...], mix_lo[...])).reshape(NS, 16, 128)
+        position = first_pos(chunk)
+        both = jnp.maximum(second_pos, position)
         lengths = jnp.concatenate([len_in[0], len_in[1]], axis=0)
         out = []
-        for i3 in range(32):
-            weight = STEP / (1.0 + 0.02 * jnp.maximum(both, i3).astype(F32))
-            alive = first_pos.astype(F32) < lengths[:, i3 : i3 + 1]
-            out.append(jnp.where(alive, turned[i3] + weight * mixed[i3], 0.0))
+        for i in range(NS):
+            weight = STEP / (1.0 + 0.02 * jnp.maximum(both, third_pos[i : i + 1]).astype(F32))
+            end = jnp.where((lane // 32) % 2 == 0, lengths[:, L3 * i : L3 * i + 1], lengths[:, L3 * i + 1 : L3 * i + 2])
+            out.append(jnp.where(position.astype(F32) < end, turned[i] + weight * mixed[i], 0.0))
         return jnp.stack(out, axis=0)
 
+    def step_1(chunk):
+        arrived(bbuf, chunk, chunk, NP)
+        z = second_line(flip_blocks(bbuf[chunk]).reshape(N, 128))
+        sbuf[chunk] = z.reshape(NS, 16, 128)
+        slab_exchange(sbuf, dbuf, chunk, CHUNKS + chunk)
+
+    def step_2(chunk):
+        arrived(dbuf, chunk, CHUNKS + chunk, NS)
+        psi = third_line(dbuf[chunk])
+        ebuf[chunk] = third_line(third_potential(psi, chunk))
+        slab_exchange(ebuf, hbuf, chunk, 2 * CHUNKS + chunk)
+
+    def step_3(chunk):
+        arrived(hbuf, chunk, 2 * CHUNKS + chunk, NS)
+        z = second_line(hbuf[chunk].reshape(N, 128))
+        gbuf[chunk] = flip_blocks(z.reshape(NP, 8, 128))
+        pencil_exchange(gbuf, rbuf, chunk, 3 * CHUNKS + chunk)
+
     for chunk in range(CHUNKS):
-        arrived(bbuf, chunk, chunk, NP)
-        z = [flip_blocks(bbuf[chunk, :, i3]).reshape(N, 128) for i3 in range(L3)]
-        z = second_line(jnp.concatenate(z, axis=1))
-        for i3 in range(L3):
-            sbuf[chunk, :, i3] = z[i3].reshape(NS, 16, 128)
-        slab_exchange(sbuf, dbuf, chunk, 2 + chunk)
-
-        arrived(dbuf, chunk, 2 + chunk, NS)
-        psi = third_line(dbuf[chunk].reshape(32, 16, 128))
-        psi = third_line(third_potential(psi, chunk))
-        ebuf[chunk] = psi.reshape(NS, L3, 16, 128)
-        slab_exchange(ebuf, hbuf, chunk, 4 + chunk)
-
-        arrived(hbuf, chunk, 4 + chunk, NS)
-        z = [hbuf[chunk, :, i3].reshape(N, 128) for i3 in range(L3)]
-        z = second_line(jnp.concatenate(z, axis=1))
-        for i3 in range(L3):
-            gbuf[chunk, :, i3] = flip_blocks(z[i3].reshape(NP, 8, 128))
-        pencil_exchange(gbuf, rbuf, chunk, 6 + chunk)
+        step_1(chunk)
+        if chunk == 0:
+
+            @pl.when(root)
+            def _():
+                len_copy(len_in.at[0], len_in.at[0], 1, (s, p)).wait_recv()
+
+            @pl.when(jnp.logical_not(root))
+            def _():
+                len_copy(len_in, len_in, 1, (s, p)).wait_recv()
+
+        else:
+            step_3(chunk - 1)
+        step_2(chunk)
+    step_3(CHUNKS - 1)
 
     out = jnp.zeros((N, 2 * N), F32)
-    for chunk in range(CHUNKS):
-        arrived(rbuf, chunk, 6 + chunk, NP)
-        r = jnp.concatenate([rbuf[chunk, :, i3].reshape(N, 128) for i3 in range(L3)], axis=1)
-        out = out + product(split2(r.T), (wf_hi[chunk], wf_lo[chunk]))
+    for half_of in range(2):
+        chunk = 2 * half_of
+        arrived(rbuf, chunk, 3 * CHUNKS + chunk, NP)
+        arrived(rbuf, chunk + 1, 3 * CHUNKS + chunk + 1, NP)
+        t0, t1 = rbuf[chunk], rbuf[chunk + 1]
+        r = [jnp.where(outer, t0, pltpu.roll(t1, 2, 1)), jnp.where(outer, pltpu.roll(t0, 6, 1), t1)]
+        r = jnp.concatenate([a.reshape(N, 128) for a in r], axis=1)
+        out = out + product(split2(r.T), (wf_hi[half_of], wf_lo[half_of]))
 
     out = potential(out[:, :N], out[:, N:])
     for part in range(2):
@@ -409,19 +457,31 @@
 
     for chunk in range(CHUNKS):
         left(ybuf, chunk, chunk, NP)
-        left(sbuf, chunk, 2 + chunk, NS)
-        left(ebuf, chunk, 4 + chunk, NS)
-        left(gbuf, chunk, 6 + chunk, NP)
+        left(sbuf, chunk, CHUNKS + chunk, NS)
+        left(ebuf, chunk, 2 * CHUNKS + chunk, NS)
+        left(gbuf, chunk, 3 * CHUNKS + chunk, NP)
+
+    @pl.when(root)
+    def _():
+        @pl.loop(0, NP - 1)
+        def _(n):
+            len_copy(len_out.at[1], len_in.at[0], 1, (s, p)).wait_send()
+
+    @pl.when(jnp.logical_not(root))
+    def _():
+        len_copy(len_out.at[0], len_col.at[0], 0, (s, p)).wait_send()
 
 
 def on_device(wavefunction, propagator, lengths, centrifugal, channel_pairs, strengths):
     shape = wavefunction.shape
     x = wavefunction.reshape(8, 2, 16, 2, 2, 128).transpose(0, 1, 2, 4, 3, 5).reshape(1024, 128)
+    operands = (x, propagator, lengths, centrifugal, channel_pairs.T, strengths.reshape(1, 32))
 
     def vmem(*dims, dtype=F32):
         return pltpu.VMEM(dims, dtype)
 
-    scratch = [
+    scratch = [pltpu.VMEM(a.shape, a.dtype) for a in operands]
+    scratch += [
         vmem(N, N),
         vmem(N, N),
         vmem(16, N),
@@ -430,44 +490,44 @@
         vmem(N, N, dtype=BF16),
         vmem(128, 128, dtype=BF16),
         vmem(128, 128, dtype=BF16),
-        vmem(CHUNKS, N, 2 * N, dtype=BF16),
-        vmem(CHUNKS, N, 2 * N, dtype=BF16),
+        vmem(2, N, 2 * N, dtype=BF16),
+        vmem(2, N, 2 * N, dtype=BF16),
         vmem(2 * N, N, dtype=BF16),
         vmem(2 * N, N, dtype=BF16),
-        vmem(CHUNKS, N, 2 * N, dtype=BF16),
-        vmem(CHUNKS, N, 2 * N, dtype=BF16),
-        vmem(CHUNKS, 32, 16, 128),
-        vmem(CHUNKS, 32, 16, 128),
+        vmem(2, N, 2 * N, dtype=BF16),
+        vmem(2, N, 2 * N, dtype=BF16),
+        vmem(CHUNKS, NS, 16, 128),
+        vmem(CHUNKS, NS, 16, 128),
         vmem(N, 2 * N, dtype=BF16),
         vmem(N, 2 * N, dtype=BF16),
         vmem(NS, 8, 128),
         vmem(2, 8, 128),
         vmem(2, 8, 128),
-        vmem(CHUNKS, NP, L3, 8, 128),
-        vmem(CHUNKS, NP, L3, 8, 128),
-        vmem(CHUNKS, NS, L3, 16, 128),
-        vmem(CHUNKS, NS, L3, 16, 128),
-        vmem(CHUNKS, NS, L3, 16, 128),
-        vmem(CHUNKS, NS, L3, 16, 128),
-        vmem(CHUNKS, NP, L3, 8, 128),
-        vmem(CHUNKS, NP, L3, 8, 128),
-        pltpu.SemaphoreType.DMA((8,)),
-        pltpu.SemaphoreType.DMA((8,)),
+        vmem(CHUNKS, NP, 8, 128),
+        vmem(CHUNKS, NP, 8, 128),
+        vmem(CHUNKS, NS, 16, 128),
+        vmem(CHUNKS, NS, 16, 128),
+        vmem(CHUNKS, NS, 16, 128),
+        vmem(CHUNKS, NS, 16, 128),
+        vmem(CHUNKS, NP, 8, 128),
+        vmem(CHUNKS, NP, 8, 128),
+        pltpu.SemaphoreType.DMA((6,)),
+        pltpu.SemaphoreType.DMA((4 * CHUNKS,)),
+        pltpu.SemaphoreType.DMA((4 * CHUNKS,)),
         pltpu.SemaphoreType.DMA((2,)),
         pltpu.SemaphoreType.DMA((2,)),
     ]
-    whole = pl.BlockSpec(memory_space=pltpu.VMEM)
     out = pl.pallas_call(
         body,
         out_shape=jax.ShapeDtypeStruct((1024, 128), F32),
-        in_specs=[whole] * 6,
-        out_specs=whole,
+        in_specs=[pl.BlockSpec(memory_space=pltpu.HBM)] * 6,
+        out_specs=pl.BlockSpec(memory_space=pltpu.VMEM),
         scratch_shapes=scratch,
         compiler_params=pltpu.CompilerParams(
-            collective_id=0, has_side_effects=True, vmem_limit_bytes=48 * 2**20
+            collective_id=0, has_side_effects=True, vmem_limit_bytes=60 * 2**20
         ),
         name="propagate",
-    )(x, propagator, lengths, centrifugal, channel_pairs.T, strengths.reshape(1, 32))
+    )(*operands)
     return out.reshape(8, 2, 16, 2, 2, 128).transpose(0, 1, 2, 4, 3, 5).reshape(shape)
 
 

time: 91.1 us -> 77 us (0.85)
  Pallas kernels: 87.2 us -> 74.8 us
  local copies, waits for them, and re-layouts: 3.58 us -> 2.06 us
    pallas_call x1, Pallas kernels: 87.2 us -> 74.8 us  [on_device(): pl.pallas_call(body, out_shape=jax.ShapeDtypeStruct((1024, 128), F32), in...]
    unnamed x13 -> x1, local copies, waits for them, and re-layouts: 3.58 us -> 2.06 us
where the time goes in v2:
time: 77 us; the launch traced here: 76.8 us
  Pallas kernels  74.8 us (97%)
  local copies, waits for them, and re-layouts  2.06 us (3%)
    pallas_call x1, Pallas kernels, on_device(): pl.pallas_call(body, out_shape=jax.ShapeDtypeStruct((1024, 128), F32), in...  74.8 us
    unnamed x1, local copies, waits for them, and re-layouts  2.06 us

profile of v2, /device:TPU:1, one launch (start us, length us, event | category | flops | bytes accessed | tf_op | source)
XLA Modules:
  0.0 76.8 jit_solution(2661187369036165272)
XLA Ops:
  0.0 74.8 %propagate.1 = f32[1024,128]{1,0:T(8,128)} custom-call(f32[1024,128]{1,0:T(8,128)} %bitcast.13, f32[2,256,256]{2,1,0:T(8,128)} %prop_hbm.1, s32[2,8]{1,0:T(2,128)} %len_hbm.1, f32[3,16]{1,0:T(4,128)} %cent_hbm.1, s32[2,32]{1,0:T(2,128)} %bitcast.14, f32[1,32]{1,0:T(1,128)} %bitcast.15), custom_call_target="tpu_custom_call" | custom-call | tf_op jit(solution)/shard_map/propagate/pallas_call | solution.py:520
  74.8 2.1 %copy.10 = f32[8,2,16,2,256]{4,3,2,1,0:T(2,128)} copy(f32[8,2,16,2,256]{4,3,2,1,0:T(2,128)} %bitcast.12) | data formatting | bytes 1048576

commit v3 on v2

--- a/solution.py
+++ b/solution.py
@@ -19,7 +19,7 @@
 L3 = 2
 C = 16
 N = 256
-CHUNKS = 4
+CHUNKS = 2
 
 
 def iota(shape, dim):
@@ -127,6 +127,20 @@
     hbuf,
     gbuf,
     rbuf,
+    cos_e,
+    sin_e,
+    wt_e,
+    len_row,
+    edge_in,
+    edge_out,
+    e_ybuf,
+    e_cbuf,
+    e_kbuf,
+    e_bbuf,
+    e_gbuf,
+    e_hbuf,
+    e_fbuf,
+    e_rbuf,
     in_sem,
     send_sem,
     recv_sem,
@@ -135,26 +149,6 @@
 ):
     p = lax.axis_index("pencil")
     s = lax.axis_index("slab")
-    barrier = pltpu.get_barrier_semaphore()
-
-    def far(n, size):
-        half = (n + 1) // 2
-        return size // 2 + (1 - 2 * (n % 2)) * half
-
-    def pencil_peer(n):
-        return lax.rem(p + far(n, NP), NP)
-
-    def slab_peer(n):
-        return lax.rem(s + far(n, NS), NS)
-
-    @pl.loop(0, NP - 1)
-    def _(n):
-        pl.semaphore_signal(barrier, inc=1, device_id=(s, pencil_peer(n)), device_id_type=MESH)
-
-    @pl.loop(0, NS - 1)
-    def _(n):
-        pl.semaphore_signal(barrier, inc=1, device_id=(slab_peer(n), p), device_id_type=MESH)
-
     pairs = [
         (pair_hbm, pair_ref),
         (str_hbm, str_ref),
@@ -166,6 +160,26 @@
     inputs = [pltpu.make_async_copy(src, dst, in_sem.at[i]) for i, (src, dst) in enumerate(pairs)]
     for item in inputs:
         item.start()
+
+    barrier = pltpu.get_barrier_semaphore()
+
+    def far(n, size):
+        half = (n + 1) // 2
+        return size // 2 + (1 - 2 * (n % 2)) * half
+
+    def pencil_peer(n):
+        return lax.rem(p + far(n, NP), NP)
+
+    def slab_peer(n):
+        return lax.rem(s + far(n, NS), NS)
+
+    @pl.loop(0, NP - 1)
+    def _(n):
+        pl.semaphore_signal(barrier, inc=1, device_id=(s, pencil_peer(n)), device_id_type=MESH)
+
+    @pl.loop(0, NS - 1)
+    def _(n):
+        pl.semaphore_signal(barrier, inc=1, device_id=(slab_peer(n), p), device_id_type=MESH)
 
     def copy(src, dst, k, device):
         return pltpu.make_async_remote_copy(
@@ -249,6 +263,7 @@
     for i3 in range(L3):
         col = column(lens[i3 : i3 + 1], L2)
         len_rows.append(col)
+        edge_out[i3] = jnp.where(lane == p, col, jnp.zeros_like(col))
         len_tile = len_tile + jnp.where(lane == L3 * s + i3, col, jnp.zeros_like(col))
     len_out[0] = len_tile
     len_a = jnp.concatenate(len_rows, axis=0)
@@ -306,11 +321,11 @@
 
     def first_line(half_of):
         y = product((w1_hi[half_of], w1_lo[half_of]), u, ((1,), (1,)))
-        y = [y[:, i * 128 : (i + 1) * 128].reshape(NP, 8, 128) for i in range(L3)]
-        ybuf[2 * half_of] = jnp.where(outer, y[0], pltpu.roll(y[1], 2, 1))
-        ybuf[2 * half_of + 1] = jnp.where(outer, pltpu.roll(y[0], 6, 1), y[1])
-
-    first_line(0)
+        return [y[:, i * 128 : (i + 1) * 128] for i in range(L3)]
+
+    y = [a.reshape(NP, 8, 128) for a in first_line(0)]
+    ybuf[0] = jnp.where(outer, y[0], pltpu.roll(y[1], 2, 1))
+    ybuf[1] = jnp.where(outer, pltpu.roll(y[0], 6, 1), y[1])
 
     root = s == p // 2
 
@@ -330,8 +345,19 @@
     def _():
         len_copy(len_out.at[0], len_col.at[s], 0, (p // 2, p)).start()
 
+    for i3 in range(L3):
+
+        @pl.when(p != L3 * s + i3)
+        def _():
+            len_copy(edge_out.at[i3], len_row.at[p], 2 + i3, (s, L3 * s + i3)).start()
+
     pencil_exchange(ybuf, bbuf, 0, 0)
-    first_line(1)
+
+    y = first_line(1)
+    for chunk in range(CHUNKS):
+        for i3 in range(L3):
+            e_ybuf[chunk, :, i3] = y[i3].reshape(NS, CHUNKS, 8, 128)[:, chunk]
+        slab_exchange(e_ybuf, e_cbuf, chunk, 4 * CHUNKS + chunk)
 
     @pl.when(root)
     def _():
@@ -346,11 +372,43 @@
         def _(n):
             len_copy(len_out.at[1], len_in.at[lax.rem(p, 2)], 1, (s, pencil_peer(n))).start()
 
-    for chunk in range(1, CHUNKS):
-        pencil_exchange(ybuf, bbuf, chunk, chunk)
+    def edge_third(x):
+        zero = jnp.zeros((2,) + x.shape[1:], F32)
+
+        def band_first(a):
+            b = jnp.concatenate([zero, a, zero], axis=0)
+            return (BAND / 24.0) * (b[:32] + b[4:36] - 16.0 * (b[1:33] + b[3:35]) + 30.0 * a)
+
+        g1 = band_first(x)
+        g2 = band_first(g1)
+        sign = jnp.where(iota((1, 8, 128), 1) < 4, 1.0, -1.0)
+        return x + sign * pltpu.roll(g1, 4, 1) - 0.5 * g2
+
+    def edge_1(chunk):
+        arrived(e_cbuf, chunk, 4 * CHUNKS + chunk, NS)
+        e_kbuf[chunk] = edge_third(e_cbuf[chunk].reshape(NP, 8, 128))
+        pencil_exchange(e_kbuf, e_bbuf, chunk, 5 * CHUNKS + chunk)
 
     re, im = prop_ref[0], prop_ref[1]
     q2_hi[...], q2_lo[...] = split2(jnp.concatenate([re, im], axis=0))
+
+    edge_1(0)
+    pencil_exchange(ybuf, bbuf, 1, 1)
+    edge_1(1)
+
+    @pl.when(root)
+    def _():
+        len_row[pl.ds(p, 1)] = edge_out[pl.ds(lax.rem(p, 2), 1)]
+        part = len_row.at[pl.ds(0, NP - 1)]
+        len_copy(part, part, 2 + lax.rem(p, 2), (s, p)).wait_recv()
+        total = jnp.sum(len_row[...], axis=0)
+        edge_out[2] = total
+        edge_in[0] = total
+
+        @pl.loop(0, NS - 1)
+        def _(n):
+            len_copy(edge_out.at[2], edge_in.at[0], 4, (slab_peer(n), p)).start()
+
     for part, (high, low) in enumerate(interleaved(re.T, -im.T)):
         wf_hi[part], wf_lo[part] = high, low
 
@@ -376,6 +434,22 @@
             c3, s3 = cos_3[i : i + 1], sin_3[i : i + 1]
             cos_d[chunk, i] = cos_12 * c3 - sin_12 * s3
             sin_d[chunk, i] = turn * (sin_12 * c3 + cos_12 * s3)
+
+    angle_2 = STEP * radial(iota((N, 128), 0), cent_row[1])
+    cos_2, sin_2 = jnp.cos(angle_2), jnp.sin(angle_2)
+    edge_rows = iota((N, 128), 0)
+
+    def edge_first_pos(chunk):
+        return 8 * (CHUNKS * s + chunk) + 4 + (lane // C) % 4
+
+    for chunk in range(CHUNKS):
+        position = edge_first_pos(chunk)
+        angle_13 = STEP * (radial(position, cent_row[0]) + radial(jnp.full((1, 128), p, jnp.int32), cent_row[2]))
+        cos_13, sin_13 = jnp.cos(angle_13), jnp.sin(angle_13)
+        cos_e[chunk] = cos_2 * cos_13 - sin_2 * sin_13
+        sin_e[chunk] = turn * (sin_2 * cos_13 + cos_2 * sin_13)
+        farthest = jnp.maximum(jnp.maximum(edge_rows, position), p).astype(F32)
+        wt_e[chunk] = STEP / (1.0 + 0.02 * farthest)
 
     q2 = (q2_hi[...], q2_lo[...])
 
@@ -419,32 +493,56 @@
         gbuf[chunk] = flip_blocks(z.reshape(NP, 8, 128))
         pencil_exchange(gbuf, rbuf, chunk, 3 * CHUNKS + chunk)
 
+    def edge_potential(psi, chunk):
+        turned = psi * cos_e[chunk] + sin_e[chunk] * pltpu.roll(psi, 64, 1)
+        mixed = product(split2(turned), (mix_hi[...], mix_lo[...]))
+        lengths = edge_in[0]
+        end = jnp.concatenate([jnp.broadcast_to(lengths[:, i : i + 1], (8, 128)) for i in range(NP)], axis=0)
+        return jnp.where(edge_first_pos(chunk).astype(F32) < end, turned + wt_e[chunk] * mixed, 0.0)
+
+    def edge_2(chunk):
+        arrived(e_bbuf, chunk, 5 * CHUNKS + chunk, NP)
+        z = second_line(flip_blocks(e_bbuf[chunk]).reshape(N, 128))
+        z = second_line(edge_potential(z, chunk))
+        e_gbuf[chunk] = flip_blocks(z.reshape(NP, 8, 128))
+        pencil_exchange(e_gbuf, e_hbuf, chunk, 6 * CHUNKS + chunk)
+
+    def edge_3(chunk):
+        arrived(e_hbuf, chunk, 6 * CHUNKS + chunk, NP)
+        e_fbuf[chunk] = edge_third(e_hbuf[chunk]).reshape(NS, L3, 8, 128)
+        slab_exchange(e_fbuf, e_rbuf, chunk, 7 * CHUNKS + chunk)
+
+    step_1(0)
+
+    @pl.when(root)
+    def _():
+        len_copy(len_in.at[0], len_in.at[0], 1, (s, p)).wait_recv()
+
+    @pl.when(jnp.logical_not(root))
+    def _():
+        len_copy(len_in, len_in, 1, (s, p)).wait_recv()
+        len_copy(edge_in, edge_in, 4, (s, p)).wait_recv()
+
+    edge_2(0)
+    step_2(0)
+    step_1(1)
+    step_3(0)
+    edge_2(1)
+    step_2(1)
+    step_3(1)
+
+    edge_3(0)
+    edge_3(1)
     for chunk in range(CHUNKS):
-        step_1(chunk)
-        if chunk == 0:
-
-            @pl.when(root)
-            def _():
-                len_copy(len_in.at[0], len_in.at[0], 1, (s, p)).wait_recv()
-
-            @pl.when(jnp.logical_not(root))
-            def _():
-                len_copy(len_in, len_in, 1, (s, p)).wait_recv()
-
-        else:
-            step_3(chunk - 1)
-        step_2(chunk)
-    step_3(CHUNKS - 1)
-
-    out = jnp.zeros((N, 2 * N), F32)
-    for half_of in range(2):
-        chunk = 2 * half_of
         arrived(rbuf, chunk, 3 * CHUNKS + chunk, NP)
-        arrived(rbuf, chunk + 1, 3 * CHUNKS + chunk + 1, NP)
-        t0, t1 = rbuf[chunk], rbuf[chunk + 1]
-        r = [jnp.where(outer, t0, pltpu.roll(t1, 2, 1)), jnp.where(outer, pltpu.roll(t0, 6, 1), t1)]
-        r = jnp.concatenate([a.reshape(N, 128) for a in r], axis=1)
-        out = out + product(split2(r.T), (wf_hi[half_of], wf_lo[half_of]))
+    t0, t1 = rbuf[0], rbuf[1]
+    r = [jnp.where(outer, t0, pltpu.roll(t1, 2, 1)), jnp.where(outer, pltpu.roll(t0, 6, 1), t1)]
+    r = jnp.concatenate([a.reshape(N, 128) for a in r], axis=1)
+    out = product(split2(r.T), (wf_hi[0], wf_lo[0]))
+    for chunk in range(CHUNKS):
+        arrived(e_rbuf, chunk, 7 * CHUNKS + chunk, NS)
+    r = [jnp.stack([e_rbuf[chunk, :, i3] for chunk in range(CHUNKS)], axis=1).reshape(N, 128) for i3 in range(L3)]
+    out = out + product(split2(jnp.concatenate(r, axis=1).T), (wf_hi[1], wf_lo[1]))
 
     out = potential(out[:, :N], out[:, N:])
     for part in range(2):
@@ -460,6 +558,10 @@
         left(sbuf, chunk, CHUNKS + chunk, NS)
         left(ebuf, chunk, 2 * CHUNKS + chunk, NS)
         left(gbuf, chunk, 3 * CHUNKS + chunk, NP)
+        left(e_ybuf, chunk, 4 * CHUNKS + chunk, NS)
+        left(e_kbuf, chunk, 5 * CHUNKS + chunk, NP)
+        left(e_gbuf, chunk, 6 * CHUNKS + chunk, NP)
+        left(e_fbuf, chunk, 7 * CHUNKS + chunk, NS)
 
     @pl.when(root)
     def _():
@@ -467,9 +569,19 @@
         def _(n):
             len_copy(len_out.at[1], len_in.at[0], 1, (s, p)).wait_send()
 
+        @pl.loop(0, NS - 1)
+        def _(n):
+            len_copy(edge_out.at[2], edge_in.at[0], 4, (s, p)).wait_send()
+
     @pl.when(jnp.logical_not(root))
     def _():
         len_copy(len_out.at[0], len_col.at[0], 0, (s, p)).wait_send()
+
+    for i3 in range(L3):
+
+        @pl.when(p != L3 * s + i3)
+        def _():
+            len_copy(edge_out.at[i3], len_row.at[0], 2 + i3, (s, p)).wait_send()
 
 
 def on_device(wavefunction, propagator, lengths, centrifugal, channel_pairs, strengths):
@@ -511,11 +623,25 @@
         vmem(CHUNKS, NS, 16, 128),
         vmem(CHUNKS, NP, 8, 128),
         vmem(CHUNKS, NP, 8, 128),
+        vmem(CHUNKS, N, 128),
+        vmem(CHUNKS, N, 128),
+        vmem(CHUNKS, N, 128),
+        vmem(NP, 8, 128),
+        vmem(1, 8, 128),
+        vmem(3, 8, 128),
+        vmem(CHUNKS, NS, L3, 8, 128),
+        vmem(CHUNKS, NS, L3, 8, 128),
+        vmem(CHUNKS, NP, 8, 128),
+        vmem(CHUNKS, NP, 8, 128),
+        vmem(CHUNKS, NP, 8, 128),
+        vmem(CHUNKS, NP, 8, 128),
+        vmem(CHUNKS, NS, L3, 8, 128),
+        vmem(CHUNKS, NS, L3, 8, 128),
         pltpu.SemaphoreType.DMA((6,)),
-        pltpu.SemaphoreType.DMA((4 * CHUNKS,)),
-        pltpu.SemaphoreType.DMA((4 * CHUNKS,)),
-        pltpu.SemaphoreType.DMA((2,)),
-        pltpu.SemaphoreType.DMA((2,)),
+        pltpu.SemaphoreType.DMA((8 * CHUNKS,)),
+        pltpu.SemaphoreType.DMA((8 * CHUNKS,)),
+        pltpu.SemaphoreType.DMA((5,)),
+        pltpu.SemaphoreType.DMA((5,)),
     ]
     out = pl.pallas_call(
         body,
@@ -524,7 +650,7 @@
         out_specs=pl.BlockSpec(memory_space=pltpu.VMEM),
         scratch_shapes=scratch,
         compiler_params=pltpu.CompilerParams(
-            collective_id=0, has_side_effects=True, vmem_limit_bytes=60 * 2**20
+            collective_id=0, has_side_effects=True, vmem_limit_bytes=53 * 2**20
         ),
         name="propagate",
     )(*operands)

time: 77 us -> 71.6 us (0.930)
  Pallas kernels: 74.8 us -> 69.9 us
    pallas_call x1, Pallas kernels: 74.8 us -> 69.9 us  [on_device(): pl.pallas_call(body, out_shape=jax.ShapeDtypeStruct((1024, 128), F32), in...]
    unnamed x1 -> x9, local copies, waits for them, and re-layouts: 2.06 us -> 1.5 us
where the time goes in v3:
time: 71.6 us; the launch traced here: 71.5 us
  Pallas kernels  69.9 us (98%)
  local copies, waits for them, and re-layouts  1.5 us (2%)
    pallas_call x1, Pallas kernels, on_device(): pl.pallas_call(body, out_shape=jax.ShapeDtypeStruct((1024, 128), F32), in...  69.9 us
    unnamed x9, local copies, waits for them, and re-layouts  1.5 us

profile of v3, /device:TPU:1, one launch (start us, length us, event | category | flops | bytes accessed | tf_op | source)
XLA Modules:
  0.0 71.5 jit_solution(15659361985410710983)
XLA Ops:
  0.0 0.0 copy-start.2
  0.0 0.0 copy-start
  0.0 0.0 copy-start.1
  0.0 0.0 copy-start.3
  0.0 0.7 copy-done.2
  0.7 0.0 copy-done
  0.7 0.0 copy-done.1
  0.7 0.0 copy-done.3
  0.7 69.9 %propagate.1 = f32[1024,128]{1,0:T(8,128)S(1)} custom-call(f32[1024,128]{1,0:T(8,128)} %bitcast.15, f32[2,256,256]{2,1,0:T(8,128)} %prop_hbm.1, s32[2,8]{1,0:T(2,128)S(1)} %copy-done.1, f32[3,16]{1,0:T(4,128)S(1)} %copy-done, s32[2,32]{1,0:T(2,128)S(1)} %bitcast.13, f32[1,32]{1,0:T(1,128)S(1)} %bitcast.14), custom_call_target="tpu_custom_call" | custom-call | tf_op jit(solution)/shard_map/propagate/pallas_call | solution.py:646
  70.7 0.8 %copy.10 = f32[8,2,16,2,256]{4,3,2,1,0:T(2,128)} copy(f32[8,2,16,2,256]{4,3,2,1,0:T(2,128)S(1)} %bitcast.12) | data formatting | bytes 1048576
Async XLA Ops:
  0.0 0.7 copy-start.2
  0.0 0.7 copy-start
  0.0 0.7 copy-start.1
  0.0 0.7 copy-start.3

commit v4 on v3

--- a/solution.py
+++ b/solution.py
@@ -70,18 +70,9 @@
 
 
 def band(x):
-    low = (iota((1, 1, 128), 2) // 32) % 2 == 0
-    swapped = jnp.where(low, pltpu.roll(x, 96, 2), pltpu.roll(x, 32, 2))
-    zero = jnp.zeros((1,) + x.shape[1:], F32)
-
-    def before(a):
-        return jnp.concatenate([zero, a[:-1]], axis=0)
-
-    def after(a):
-        return jnp.concatenate([a[1:], zero], axis=0)
-
-    inner = swapped + jnp.where(low, before(swapped), after(swapped))
-    return (BAND / 24.0) * (before(x) + after(x) - 16.0 * inner + 30.0 * x)
+    zero = jnp.zeros((2,) + x.shape[1:], F32)
+    y = jnp.concatenate([zero, x, zero], axis=0)
+    return (BAND / 24.0) * (y[:32] + y[4:36] - 16.0 * (y[1:33] + y[3:35]) + 30.0 * x)
 
 
 def body(
@@ -317,15 +308,13 @@
     for part, (high, low) in enumerate(interleaved(prop_ref[0], prop_ref[1])):
         w1_hi[part], w1_lo[part] = high, low
 
-    outer = (iota((1, 8, 128), 1) // 2) % 2 == 0
-
     def first_line(half_of):
         y = product((w1_hi[half_of], w1_lo[half_of]), u, ((1,), (1,)))
         return [y[:, i * 128 : (i + 1) * 128] for i in range(L3)]
 
-    y = [a.reshape(NP, 8, 128) for a in first_line(0)]
-    ybuf[0] = jnp.where(outer, y[0], pltpu.roll(y[1], 2, 1))
-    ybuf[1] = jnp.where(outer, pltpu.roll(y[0], 6, 1), y[1])
+    y = first_line(0)
+    for i3 in range(L3):
+        ybuf[0, :, i3] = y[i3].reshape(NP, 8, 128)
 
     root = s == p // 2
 
@@ -357,7 +346,7 @@
     for chunk in range(CHUNKS):
         for i3 in range(L3):
             e_ybuf[chunk, :, i3] = y[i3].reshape(NS, CHUNKS, 8, 128)[:, chunk]
-        slab_exchange(e_ybuf, e_cbuf, chunk, 4 * CHUNKS + chunk)
+        slab_exchange(e_ybuf, e_cbuf, chunk, 4 + chunk)
 
     @pl.when(root)
     def _():
@@ -373,27 +362,20 @@
             len_copy(len_out.at[1], len_in.at[lax.rem(p, 2)], 1, (s, pencil_peer(n))).start()
 
     def edge_third(x):
-        zero = jnp.zeros((2,) + x.shape[1:], F32)
-
-        def band_first(a):
-            b = jnp.concatenate([zero, a, zero], axis=0)
-            return (BAND / 24.0) * (b[:32] + b[4:36] - 16.0 * (b[1:33] + b[3:35]) + 30.0 * a)
-
-        g1 = band_first(x)
-        g2 = band_first(g1)
+        g1 = band(x)
+        g2 = band(g1)
         sign = jnp.where(iota((1, 8, 128), 1) < 4, 1.0, -1.0)
         return x + sign * pltpu.roll(g1, 4, 1) - 0.5 * g2
 
     def edge_1(chunk):
-        arrived(e_cbuf, chunk, 4 * CHUNKS + chunk, NS)
+        arrived(e_cbuf, chunk, 4 + chunk, NS)
         e_kbuf[chunk] = edge_third(e_cbuf[chunk].reshape(NP, 8, 128))
-        pencil_exchange(e_kbuf, e_bbuf, chunk, 5 * CHUNKS + chunk)
+        pencil_exchange(e_kbuf, e_bbuf, chunk, 6 + chunk)
 
     re, im = prop_ref[0], prop_ref[1]
     q2_hi[...], q2_lo[...] = split2(jnp.concatenate([re, im], axis=0))
 
     edge_1(0)
-    pencil_exchange(ybuf, bbuf, 1, 1)
     edge_1(1)
 
     @pl.when(root)
@@ -418,22 +400,19 @@
     ]
     lane = iota((1, 128), 1)
     second_pos = 16 * s + iota((16, 128), 0)
-    third_pos = L3 * iota((NS, 128), 0) + (lane // 32) % 2
-
-    def first_pos(chunk):
-        return 8 * p + 2 * chunk + (lane // C) % 2
+    third_pos = iota((32, 128), 0)
+    first_pos = 8 * p + (lane // C) % 4
 
     angle_2 = STEP * radial(second_pos, cent_row[1])
     angle_3 = STEP * radial(third_pos, cent_row[2])
     cos_3, sin_3 = jnp.cos(angle_3), jnp.sin(angle_3)
     turn = jnp.where(lane < 64, 1.0, -1.0)
-    for chunk in range(CHUNKS):
-        angle_12 = angle_2 + STEP * radial(first_pos(chunk), cent_row[0])
-        cos_12, sin_12 = jnp.cos(angle_12), jnp.sin(angle_12)
-        for i in range(NS):
-            c3, s3 = cos_3[i : i + 1], sin_3[i : i + 1]
-            cos_d[chunk, i] = cos_12 * c3 - sin_12 * s3
-            sin_d[chunk, i] = turn * (sin_12 * c3 + cos_12 * s3)
+    angle_12 = angle_2 + STEP * radial(first_pos, cent_row[0])
+    cos_12, sin_12 = jnp.cos(angle_12), jnp.sin(angle_12)
+    for i in range(32):
+        c3, s3 = cos_3[i : i + 1], sin_3[i : i + 1]
+        cos_d[i] = cos_12 * c3 - sin_12 * s3
+        sin_d[i] = turn * (sin_12 * c3 + cos_12 * s3)
 
     angle_2 = STEP * radial(iota((N, 128), 0), cent_row[1])
     cos_2, sin_2 = jnp.cos(angle_2), jnp.sin(angle_2)
@@ -462,36 +441,42 @@
         g2 = band(g1)
         return psi + turn * pltpu.roll(g1, 64, 2) - 0.5 * g2
 
-    def third_potential(psi, chunk):
-        turned = psi * cos_d[chunk] + sin_d[chunk] * pltpu.roll(psi, 64, 2)
-        mixed = product(split2(turned.reshape(N, 128)), (mix_hi[...], mix_lo[...])).reshape(NS, 16, 128)
-        position = first_pos(chunk)
-        both = jnp.maximum(second_pos, position)
+    def third_potential(psi):
+        turned = psi * cos_d[...] + sin_d[...] * pltpu.roll(psi, 64, 2)
+        mixed = product(split2(turned.reshape(512, 128)), (mix_hi[...], mix_lo[...])).reshape(32, 16, 128)
+        both = jnp.maximum(second_pos, first_pos)
         lengths = jnp.concatenate([len_in[0], len_in[1]], axis=0)
         out = []
-        for i in range(NS):
-            weight = STEP / (1.0 + 0.02 * jnp.maximum(both, third_pos[i : i + 1]).astype(F32))
-            end = jnp.where((lane // 32) % 2 == 0, lengths[:, L3 * i : L3 * i + 1], lengths[:, L3 * i + 1 : L3 * i + 2])
-            out.append(jnp.where(position.astype(F32) < end, turned[i] + weight * mixed[i], 0.0))
+        for i in range(32):
+            weight = STEP / (1.0 + 0.02 * jnp.maximum(both, i).astype(F32))
+            alive = first_pos.astype(F32) < lengths[:, i : i + 1]
+            out.append(jnp.where(alive, turned[i] + weight * mixed[i], 0.0))
         return jnp.stack(out, axis=0)
 
-    def step_1(chunk):
-        arrived(bbuf, chunk, chunk, NP)
-        z = second_line(flip_blocks(bbuf[chunk]).reshape(N, 128))
-        sbuf[chunk] = z.reshape(NS, 16, 128)
-        slab_exchange(sbuf, dbuf, chunk, CHUNKS + chunk)
-
-    def step_2(chunk):
-        arrived(dbuf, chunk, CHUNKS + chunk, NS)
-        psi = third_line(dbuf[chunk])
-        ebuf[chunk] = third_line(third_potential(psi, chunk))
-        slab_exchange(ebuf, hbuf, chunk, 2 * CHUNKS + chunk)
-
-    def step_3(chunk):
-        arrived(hbuf, chunk, 2 * CHUNKS + chunk, NS)
-        z = second_line(hbuf[chunk].reshape(N, 128))
-        gbuf[chunk] = flip_blocks(z.reshape(NP, 8, 128))
-        pencil_exchange(gbuf, rbuf, chunk, 3 * CHUNKS + chunk)
+    def second_pair(z):
+        both = product(q2, split2(jnp.concatenate(z, axis=1)))
+        both = [both[:, i * 128 : (i + 1) * 128] for i in range(L3)]
+        return [b[:N] - turn * pltpu.roll(b[N:], 64, 1) for b in both]
+
+    def step_1():
+        arrived(bbuf, 0, 0, NP)
+        z = second_pair([flip_blocks(bbuf[0, :, i3]).reshape(N, 128) for i3 in range(L3)])
+        for i3 in range(L3):
+            sbuf[0, :, i3] = z[i3].reshape(NS, 16, 128)
+        slab_exchange(sbuf, dbuf, 0, 1)
+
+    def step_2():
+        arrived(dbuf, 0, 1, NS)
+        psi = third_line(dbuf[0].reshape(32, 16, 128))
+        ebuf[0] = third_line(third_potential(psi)).reshape(NS, L3, 16, 128)
+        slab_exchange(ebuf, hbuf, 0, 2)
+
+    def step_3():
+        arrived(hbuf, 0, 2, NS)
+        z = second_pair([hbuf[0, :, i3].reshape(N, 128) for i3 in range(L3)])
+        for i3 in range(L3):
+            gbuf[0, :, i3] = flip_blocks(z[i3].reshape(NP, 8, 128))
+        pencil_exchange(gbuf, rbuf, 0, 3)
 
     def edge_potential(psi, chunk):
         turned = psi * cos_e[chunk] + sin_e[chunk] * pltpu.roll(psi, 64, 1)
@@ -501,18 +486,18 @@
         return jnp.where(edge_first_pos(chunk).astype(F32) < end, turned + wt_e[chunk] * mixed, 0.0)
 
     def edge_2(chunk):
-        arrived(e_bbuf, chunk, 5 * CHUNKS + chunk, NP)
+        arrived(e_bbuf, chunk, 6 + chunk, NP)
         z = second_line(flip_blocks(e_bbuf[chunk]).reshape(N, 128))
         z = second_line(edge_potential(z, chunk))
         e_gbuf[chunk] = flip_blocks(z.reshape(NP, 8, 128))
-        pencil_exchange(e_gbuf, e_hbuf, chunk, 6 * CHUNKS + chunk)
+        pencil_exchange(e_gbuf, e_hbuf, chunk, 8 + chunk)
 
     def edge_3(chunk):
-        arrived(e_hbuf, chunk, 6 * CHUNKS + chunk, NP)
+        arrived(e_hbuf, chunk, 8 + chunk, NP)
         e_fbuf[chunk] = edge_third(e_hbuf[chunk]).reshape(NS, L3, 8, 128)
-        slab_exchange(e_fbuf, e_rbuf, chunk, 7 * CHUNKS + chunk)
-
-    step_1(0)
+        slab_exchange(e_fbuf, e_rbuf, chunk, 10 + chunk)
+
+    step_1()
 
     @pl.when(root)
     def _():
@@ -524,25 +509,19 @@
         len_copy(edge_in, edge_in, 4, (s, p)).wait_recv()
 
     edge_2(0)
-    step_2(0)
-    step_1(1)
-    step_3(0)
+    step_2()
     edge_2(1)
-    step_2(1)
-    step_3(1)
+    step_3()
 
     edge_3(0)
     edge_3(1)
     for chunk in range(CHUNKS):
-        arrived(rbuf, chunk, 3 * CHUNKS + chunk, NP)
-    t0, t1 = rbuf[0], rbuf[1]
-    r = [jnp.where(outer, t0, pltpu.roll(t1, 2, 1)), jnp.where(outer, pltpu.roll(t0, 6, 1), t1)]
-    r = jnp.concatenate([a.reshape(N, 128) for a in r], axis=1)
-    out = product(split2(r.T), (wf_hi[0], wf_lo[0]))
-    for chunk in range(CHUNKS):
-        arrived(e_rbuf, chunk, 7 * CHUNKS + chunk, NS)
+        arrived(e_rbuf, chunk, 10 + chunk, NS)
     r = [jnp.stack([e_rbuf[chunk, :, i3] for chunk in range(CHUNKS)], axis=1).reshape(N, 128) for i3 in range(L3)]
-    out = out + product(split2(jnp.concatenate(r, axis=1).T), (wf_hi[1], wf_lo[1]))
+    out = product(split2(jnp.concatenate(r, axis=1).T), (wf_hi[1], wf_lo[1]))
+    arrived(rbuf, 0, 3, NP)
+    r = jnp.concatenate([rbuf[0, :, i3].reshape(N, 128) for i3 in range(L3)], axis=1)
+    out = out + product(split2(r.T), (wf_hi[0], wf_lo[0]))
 
     out = potential(out[:, :N], out[:, N:])
     for part in range(2):
@@ -553,15 +532,15 @@
                 for l in range(2):
                     o_ref[pl.ds(base + 2 * l, C, stride=4), :] = out[part][start : start + C, l * 128 : (l + 1) * 128]
 
+    left(ybuf, 0, 0, NP)
+    left(sbuf, 0, 1, NS)
+    left(ebuf, 0, 2, NS)
+    left(gbuf, 0, 3, NP)
     for chunk in range(CHUNKS):
-        left(ybuf, chunk, chunk, NP)
-        left(sbuf, chunk, CHUNKS + chunk, NS)
-        left(ebuf, chunk, 2 * CHUNKS + chunk, NS)
-        left(gbuf, chunk, 3 * CHUNKS + chunk, NP)
-        left(e_ybuf, chunk, 4 * CHUNKS + chunk, NS)
-        left(e_kbuf, chunk, 5 * CHUNKS + chunk, NP)
-        left(e_gbuf, chunk, 6 * CHUNKS + chunk, NP)
-        left(e_fbuf, chunk, 7 * CHUNKS + chunk, NS)
+        left(e_ybuf, chunk, 4 + chunk, NS)
+        left(e_kbuf, chunk, 6 + chunk, NP)
+        left(e_gbuf, chunk, 8 + chunk, NP)
+        left(e_fbuf, chunk, 10 + chunk, NS)
 
     @pl.when(root)
     def _():
@@ -608,21 +587,21 @@
         vmem(2 * N, N, dtype=BF16),
         vmem(2, N, 2 * N, dtype=BF16),
         vmem(2, N, 2 * N, dtype=BF16),
-        vmem(CHUNKS, NS, 16, 128),
-        vmem(CHUNKS, NS, 16, 128),
+        vmem(32, 16, 128),
+        vmem(32, 16, 128),
         vmem(N, 2 * N, dtype=BF16),
         vmem(N, 2 * N, dtype=BF16),
         vmem(NS, 8, 128),
         vmem(2, 8, 128),
         vmem(2, 8, 128),
-        vmem(CHUNKS, NP, 8, 128),
-        vmem(CHUNKS, NP, 8, 128),
-        vmem(CHUNKS, NS, 16, 128),
-        vmem(CHUNKS, NS, 16, 128),
-        vmem(CHUNKS, NS, 16, 128),
-        vmem(CHUNKS, NS, 16, 128),
-        vmem(CHUNKS, NP, 8, 128),
-        vmem(CHUNKS, NP, 8, 128),
+        vmem(1, NP, L3, 8, 128),
+        vmem(1, NP, L3, 8, 128),
+        vmem(1, NS, L3, 16, 128),
+        vmem(1, NS, L3, 16, 128),
+        vmem(1, NS, L3, 16, 128),
+        vmem(1, NS, L3, 16, 128),
+        vmem(1, NP, L3, 8, 128),
+        vmem(1, NP, L3, 8, 128),
         vmem(CHUNKS, N, 128),
         vmem(CHUNKS, N, 128),
         vmem(CHUNKS, N, 128),
@@ -638,8 +617,8 @@
         vmem(CHUNKS, NS, L3, 8, 128),
         vmem(CHUNKS, NS, L3, 8, 128),
         pltpu.SemaphoreType.DMA((6,)),
-        pltpu.SemaphoreType.DMA((8 * CHUNKS,)),
-        pltpu.SemaphoreType.DMA((8 * CHUNKS,)),
+        pltpu.SemaphoreType.DMA((12,)),
+        pltpu.SemaphoreType.DMA((12,)),
         pltpu.SemaphoreType.DMA((5,)),
         pltpu.SemaphoreType.DMA((5,)),
     ]

time: 71.6 us -> 69 us (0.964)
  Pallas kernels: 69.9 us -> 67.4 us
    pallas_call x1, Pallas kernels: 69.9 us -> 67.4 us  [on_device(): pl.pallas_call(body, out_shape=jax.ShapeDtypeStruct((1024, 128), F32), in...]
where the time goes in v4:
time: 69 us; the launch traced here: 68.9 us
  Pallas kernels  67.4 us (98%)
  local copies, waits for them, and re-layouts  1.5 us (2%)
    pallas_call x1, Pallas kernels, on_device(): pl.pallas_call(body, out_shape=jax.ShapeDtypeStruct((1024, 128), F32), in...  67.4 us
    unnamed x9, local copies, waits for them, and re-layouts  1.5 us

profile of v4, /device:TPU:1, one launch (start us, length us, event | category | flops | bytes accessed | tf_op | source)
XLA Modules:
  0.0 68.9 jit_solution(17680226934924630288)
XLA Ops:
  0.0 0.0 copy-start.2
  0.0 0.0 copy-start
  0.0 0.0 copy-start.1
  0.0 0.0 copy-start.3
  0.0 0.7 copy-done.2
  0.7 0.0 copy-done
  0.7 0.0 copy-done.1
  0.7 0.0 copy-done.3
  0.7 67.4 %propagate.1 = f32[1024,128]{1,0:T(8,128)S(1)} custom-call(f32[1024,128]{1,0:T(8,128)} %bitcast.15, f32[2,256,256]{2,1,0:T(8,128)} %prop_hbm.1, s32[2,8]{1,0:T(2,128)S(1)} %copy-done.1, f32[3,16]{1,0:T(4,128)S(1)} %copy-done, s32[2,32]{1,0:T(2,128)S(1)} %bitcast.13, f32[1,32]{1,0:T(1,128)S(1)} %bitcast.14), custom_call_target="tpu_custom_call" | custom-call | tf_op jit(solution)/shard_map/propagate/pallas_call | solution.py:625
  68.1 0.8 %copy.10 = f32[8,2,16,2,256]{4,3,2,1,0:T(2,128)} copy(f32[8,2,16,2,256]{4,3,2,1,0:T(2,128)S(1)} %bitcast.12) | data formatting | bytes 1048576
Async XLA Ops:
  0.0 0.7 copy-start.2
  0.0 0.7 %copy-start = (f32[3,16]{1,0:T(4,128)S(1)}, f32[3,16]{1,0:T(4,128)}, u32[]{:S(2)}) copy-start(f32[3,16]{1,0:T(4,128)} %cent_hbm.1) | copy-start | bytes 580
  0.0 0.7 %copy-start.1 = (s32[2,8]{1,0:T(2,128)S(1)}, s32[2,8]{1,0:T(2,128)}, u32[]{:S(2)}) copy-start(s32[2,8]{1,0:T(2,128)} %len_hbm.1) | copy-start | bytes 196
  0.0 0.7 %copy-start.3 = (f32[32]{0:T(128)S(1)}, f32[32]{0:T(128)}, u32[]{:S(2)}) copy-start(f32[32]{0:T(128)} %param.11) | copy-start | bytes 388

commit v5 on v4

--- a/solution.py
+++ b/solution.py
@@ -95,8 +95,7 @@
     lv_a,
     kron_hi,
     kron_lo,
-    mix_hi,
-    mix_lo,
+    mix,
     w1_hi,
     w1_lo,
     q2_hi,
@@ -140,6 +139,26 @@
 ):
     p = lax.axis_index("pencil")
     s = lax.axis_index("slab")
+    barrier = pltpu.get_barrier_semaphore()
+
+    def far(n, size):
+        half = (n + 1) // 2
+        return size // 2 + (1 - 2 * (n % 2)) * half
+
+    def pencil_peer(n):
+        return lax.rem(p + far(n, NP), NP)
+
+    def slab_peer(n):
+        return lax.rem(s + far(n, NS), NS)
+
+    @pl.loop(0, NP - 1)
+    def _(n):
+        pl.semaphore_signal(barrier, inc=1, device_id=(s, pencil_peer(n)), device_id_type=MESH)
+
+    @pl.loop(0, NS - 1)
+    def _(n):
+        pl.semaphore_signal(barrier, inc=1, device_id=(slab_peer(n), p), device_id_type=MESH)
+
     pairs = [
         (pair_hbm, pair_ref),
         (str_hbm, str_ref),
@@ -152,26 +171,6 @@
     for item in inputs:
         item.start()
 
-    barrier = pltpu.get_barrier_semaphore()
-
-    def far(n, size):
-        half = (n + 1) // 2
-        return size // 2 + (1 - 2 * (n % 2)) * half
-
-    def pencil_peer(n):
-        return lax.rem(p + far(n, NP), NP)
-
-    def slab_peer(n):
-        return lax.rem(s + far(n, NS), NS)
-
-    @pl.loop(0, NP - 1)
-    def _(n):
-        pl.semaphore_signal(barrier, inc=1, device_id=(s, pencil_peer(n)), device_id_type=MESH)
-
-    @pl.loop(0, NS - 1)
-    def _(n):
-        pl.semaphore_signal(barrier, inc=1, device_id=(slab_peer(n), p), device_id_type=MESH)
-
     def copy(src, dst, k, device):
         return pltpu.make_async_remote_copy(
             src_ref=src,
@@ -230,7 +229,9 @@
     row, col = iota((128, 128), 0), iota((128, 128), 1)
     same = (row // C) % 4 == (col // C) % 4
     sign = (row // 64 - col // 64).astype(F32)
-    mix_hi[...], mix_lo[...] = split2(jnp.where(same, tiled[:128, :128] * sign, 0.0))
+    high, low = split2(jnp.where(same, tiled[:128, :128] * sign, 0.0))
+    mix[:128, :128], mix[:128, 128:] = high, low
+    mix[128:, :128], mix[128:, 128:] = high, jnp.zeros_like(low)
 
     inputs[2].wait()
     inputs[3].wait()
@@ -268,15 +269,16 @@
     inputs[4].wait()
     kron = (kron_hi[...], kron_lo[...])
 
-    def potential(re, im):
-        cosine, sine = cos_a[...], sin_a[...]
+    def potential(re, im, kron, start, count):
+        rows_of = slice(start * C, (start + count) * C)
+        cosine, sine = cos_a[rows_of], sin_a[rows_of]
         turned_re = re * cosine + im * sine
         turned_im = im * cosine - re * sine
         mixed_re = product(kron, split2(turned_im))
         mixed_im = product(kron, split2(turned_re))
 
         def rows(a):
-            return jnp.concatenate([jnp.broadcast_to(a[m : m + 1], (C, N)) for m in range(16)], axis=0)
+            return jnp.concatenate([jnp.broadcast_to(a[m : m + 1], (C, N)) for m in range(start, start + count)], axis=0)
 
         weight, alive = rows(wl_a[...]), rows(lv_a[...])
         return turned_re * alive + weight * mixed_re, turned_im * alive - weight * mixed_im
@@ -291,7 +293,7 @@
                 )
         return jnp.concatenate(blocks, axis=0)
 
-    v_re, v_im = potential(load(0), load(1))
+    v_re, v_im = potential(load(0), load(1), kron, 0, 16)
     u_hi[...], u_lo[...] = split2(jnp.concatenate([v_re, v_im], axis=1))
     u = (u_hi[...], u_lo[...])
 
@@ -433,8 +435,14 @@
     q2 = (q2_hi[...], q2_lo[...])
 
     def second_line(z):
-        both = product(q2, split2(z))
+        high, low = split2(z)
+        both = jnp.dot(q2[0], jnp.concatenate([high, low], axis=1), preferred_element_type=F32)
+        both = both[:, :128] + both[:, 128:] + jnp.dot(q2[1], high, preferred_element_type=F32)
         return both[:N] - turn * pltpu.roll(both[N:], 64, 1)
+
+    def mixture(turned):
+        both = jnp.dot(jnp.concatenate(split2(turned), axis=1), mix[...], preferred_element_type=F32)
+        return both[:, :128] + both[:, 128:]
 
     def third_line(psi):
         g1 = band(psi)
@@ -443,7 +451,7 @@
 
     def third_potential(psi):
         turned = psi * cos_d[...] + sin_d[...] * pltpu.roll(psi, 64, 2)
-        mixed = product(split2(turned.reshape(512, 128)), (mix_hi[...], mix_lo[...])).reshape(32, 16, 128)
+        mixed = mixture(turned.reshape(512, 128)).reshape(32, 16, 128)
         both = jnp.maximum(second_pos, first_pos)
         lengths = jnp.concatenate([len_in[0], len_in[1]], axis=0)
         out = []
@@ -480,7 +488,7 @@
 
     def edge_potential(psi, chunk):
         turned = psi * cos_e[chunk] + sin_e[chunk] * pltpu.roll(psi, 64, 1)
-        mixed = product(split2(turned), (mix_hi[...], mix_lo[...]))
+        mixed = mixture(turned)
         lengths = edge_in[0]
         end = jnp.concatenate([jnp.broadcast_to(lengths[:, i : i + 1], (8, 128)) for i in range(NP)], axis=0)
         return jnp.where(edge_first_pos(chunk).astype(F32) < end, turned + wt_e[chunk] * mixed, 0.0)
@@ -518,19 +526,18 @@
     for chunk in range(CHUNKS):
         arrived(e_rbuf, chunk, 10 + chunk, NS)
     r = [jnp.stack([e_rbuf[chunk, :, i3] for chunk in range(CHUNKS)], axis=1).reshape(N, 128) for i3 in range(L3)]
-    out = product(split2(jnp.concatenate(r, axis=1).T), (wf_hi[1], wf_lo[1]))
+    wf = [(wf_hi[k], wf_lo[k]) for k in range(2)]
+    early = [product(split2(a.T), wf[1]) for a in r]
     arrived(rbuf, 0, 3, NP)
-    r = jnp.concatenate([rbuf[0, :, i3].reshape(N, 128) for i3 in range(L3)], axis=1)
-    out = out + product(split2(r.T), (wf_hi[0], wf_lo[0]))
-
-    out = potential(out[:, :N], out[:, N:])
-    for part in range(2):
-        for i3 in range(L3):
+    block = (kron_hi[:128, :128], kron_lo[:128, :128])
+    for i3 in range(L3):
+        out = early[i3] + product(split2(rbuf[0, :, i3].reshape(N, 128).T), wf[0])
+        out = potential(out[:, :N], out[:, N:], block, i3 * L2, L2)
+        for part in range(2):
             for i2 in range(L2):
                 base = (i2 * 2 + part) * 64 + i3
-                start = (i3 * L2 + i2) * C
                 for l in range(2):
-                    o_ref[pl.ds(base + 2 * l, C, stride=4), :] = out[part][start : start + C, l * 128 : (l + 1) * 128]
+                    o_ref[pl.ds(base + 2 * l, C, stride=4), :] = out[part][i2 * C : (i2 + 1) * C, l * 128 : (l + 1) * 128]
 
     left(ybuf, 0, 0, NP)
     left(sbuf, 0, 1, NS)
@@ -579,8 +586,7 @@
         vmem(16, N),
         vmem(N, N, dtype=BF16),
         vmem(N, N, dtype=BF16),
-        vmem(128, 128, dtype=BF16),
-        vmem(128, 128, dtype=BF16),
+        vmem(N, N, dtype=BF16),
         vmem(2, N, 2 * N, dtype=BF16),
         vmem(2, N, 2 * N, dtype=BF16),
         vmem(2 * N, N, dtype=BF16),

time: 69 us -> 68.5 us (level)
  no operation moved by 1% of the time
where the time goes in v5:
time: 68.5 us; the launch traced here: 68.4 us
  Pallas kernels  66.9 us (98%)
  local copies, waits for them, and re-layouts  1.5 us (2%)
    pallas_call x1, Pallas kernels, on_device(): pl.pallas_call(body, out_shape=jax.ShapeDtypeStruct((1024, 128), F32), in...  66.9 us
    unnamed x9, local copies, waits for them, and re-layouts  1.5 us

profile of v5, /device:TPU:1, one launch (start us, length us, event | category | flops | bytes accessed | tf_op | source)
XLA Modules:
  0.0 68.4 jit_solution(9294505091815934457)
XLA Ops:
  0.0 0.0 copy-start.2
  0.0 0.0 copy-start
  0.0 0.0 copy-start.1
  0.0 0.0 copy-start.3
  0.0 0.7 copy-done.2
  0.7 0.0 copy-done
  0.7 0.0 copy-done.1
  0.7 0.0 copy-done.3
  0.7 66.9 %propagate.1 = f32[1024,128]{1,0:T(8,128)S(1)} custom-call(f32[1024,128]{1,0:T(8,128)} %bitcast.15, f32[2,256,256]{2,1,0:T(8,128)} %prop_hbm.1, s32[2,8]{1,0:T(2,128)S(1)} %copy-done.1, f32[3,16]{1,0:T(4,128)S(1)} %copy-done, s32[2,32]{1,0:T(2,128)S(1)} %bitcast.13, f32[1,32]{1,0:T(1,128)S(1)} %bitcast.14), custom_call_target="tpu_custom_call" | custom-call | tf_op jit(solution)/shard_map/propagate/pallas_call | solution.py:631
  67.6 0.8 %copy.10 = f32[8,2,16,2,256]{4,3,2,1,0:T(2,128)} copy(f32[8,2,16,2,256]{4,3,2,1,0:T(2,128)S(1)} %bitcast.12) | data formatting | bytes 1048576
Async XLA Ops:
  0.0 0.7 copy-start.2
  0.0 0.7 %copy-start = (f32[3,16]{1,0:T(4,128)S(1)}, f32[3,16]{1,0:T(4,128)}, u32[]{:S(2)}) copy-start(f32[3,16]{1,0:T(4,128)} %cent_hbm.1) | copy-start | bytes 580
  0.0 0.7 %copy-start.1 = (s32[2,8]{1,0:T(2,128)S(1)}, s32[2,8]{1,0:T(2,128)}, u32[]{:S(2)}) copy-start(s32[2,8]{1,0:T(2,128)} %len_hbm.1) | copy-start | bytes 196
  0.0 0.7 %copy-start.3 = (f32[32]{0:T(128)S(1)}, f32[32]{0:T(128)}, u32[]{:S(2)}) copy-start(f32[32]{0:T(128)} %param.11) | copy-start | bytes 388

commit v6 on v5

--- a/solution.py
+++ b/solution.py
@@ -120,6 +120,7 @@
     cos_e,
     sin_e,
     wt_e,
+    lv_e,
     len_row,
     edge_in,
     edge_out,
@@ -269,13 +270,23 @@
     inputs[4].wait()
     kron = (kron_hi[...], kron_lo[...])
 
+    def coupled(kron, turned):
+        high, low = split2(turned)
+        if kron[0].shape[1] == N:
+            return product(kron, (high, low))
+        top = jnp.concatenate([high, low], axis=1)
+        bottom = jnp.concatenate([high, jnp.zeros_like(low)], axis=1)
+        left_side = jnp.concatenate(kron, axis=1)
+        both = jnp.dot(left_side, jnp.concatenate([top, bottom], axis=0), preferred_element_type=F32)
+        return both[:, :N] + both[:, N:]
+
     def potential(re, im, kron, start, count):
         rows_of = slice(start * C, (start + count) * C)
         cosine, sine = cos_a[rows_of], sin_a[rows_of]
         turned_re = re * cosine + im * sine
         turned_im = im * cosine - re * sine
-        mixed_re = product(kron, split2(turned_im))
-        mixed_im = product(kron, split2(turned_re))
+        mixed_re = coupled(kron, turned_im)
+        mixed_im = coupled(kron, turned_re)
 
         def rows(a):
             return jnp.concatenate([jnp.broadcast_to(a[m : m + 1], (C, N)) for m in range(start, start + count)], axis=0)
@@ -330,24 +341,26 @@
             device_id_type=MESH,
         )
 
-    pl.semaphore_wait(barrier, NP + NS - 2)
-
-    @pl.when(jnp.logical_not(root))
-    def _():
-        len_copy(len_out.at[0], len_col.at[s], 0, (p // 2, p)).start()
-
-    for i3 in range(L3):
-
-        @pl.when(p != L3 * s + i3)
-        def _():
-            len_copy(edge_out.at[i3], len_row.at[p], 2 + i3, (s, L3 * s + i3)).start()
-
-    pencil_exchange(ybuf, bbuf, 0, 0)
-
     y = first_line(1)
     for chunk in range(CHUNKS):
         for i3 in range(L3):
             e_ybuf[chunk, :, i3] = y[i3].reshape(NS, CHUNKS, 8, 128)[:, chunk]
+
+    pl.semaphore_wait(barrier, NP + NS - 2)
+
+    @pl.when(jnp.logical_not(root))
+    def _():
+        len_copy(len_out.at[0], len_col.at[s], 0, (p // 2, p)).start()
+
+    for i3 in range(L3):
+
+        @pl.when(p != L3 * s + i3)
+        def _():
+            len_copy(edge_out.at[i3], len_row.at[p], 2 + i3, (s, L3 * s + i3)).start()
+
+    pencil_exchange(ybuf, bbuf, 0, 0)
+
+    for chunk in range(CHUNKS):
         slab_exchange(e_ybuf, e_cbuf, chunk, 4 + chunk)
 
     @pl.when(root)
@@ -489,9 +502,7 @@
     def edge_potential(psi, chunk):
         turned = psi * cos_e[chunk] + sin_e[chunk] * pltpu.roll(psi, 64, 1)
         mixed = mixture(turned)
-        lengths = edge_in[0]
-        end = jnp.concatenate([jnp.broadcast_to(lengths[:, i : i + 1], (8, 128)) for i in range(NP)], axis=0)
-        return jnp.where(edge_first_pos(chunk).astype(F32) < end, turned + wt_e[chunk] * mixed, 0.0)
+        return lv_e[chunk] * turned + wt_e[chunk] * mixed
 
     def edge_2(chunk):
         arrived(e_bbuf, chunk, 6 + chunk, NP)
@@ -515,6 +526,13 @@
     def _():
         len_copy(len_in, len_in, 1, (s, p)).wait_recv()
         len_copy(edge_in, edge_in, 4, (s, p)).wait_recv()
+
+    lengths = edge_in[0]
+    end = jnp.concatenate([jnp.broadcast_to(lengths[:, i : i + 1], (8, 128)) for i in range(NP)], axis=0)
+    for chunk in range(CHUNKS):
+        alive = (edge_first_pos(chunk).astype(F32) < end).astype(F32)
+        lv_e[chunk] = alive
+        wt_e[chunk] = alive * wt_e[chunk]
 
     edge_2(0)
     step_2()
@@ -611,6 +629,7 @@
         vmem(CHUNKS, N, 128),
         vmem(CHUNKS, N, 128),
         vmem(CHUNKS, N, 128),
+        vmem(CHUNKS, N, 128),
         vmem(NP, 8, 128),
         vmem(1, 8, 128),
         vmem(3, 8, 128),

time: 68.5 us -> 68.3 us (level)
  no operation moved by 1% of the time
where the time goes in v6:
time: 68.3 us; the launch traced here: 68.2 us
  Pallas kernels  66.7 us (98%)
  local copies, waits for them, and re-layouts  1.5 us (2%)
    pallas_call x1, Pallas kernels, on_device(): pl.pallas_call(body, out_shape=jax.ShapeDtypeStruct((1024, 128), F32), in...  66.7 us
    unnamed x9, local copies, waits for them, and re-layouts  1.5 us

profile of v6, /device:TPU:1, one launch (start us, length us, event | category | flops | bytes accessed | tf_op | source)
XLA Modules:
  0.0 68.2 jit_solution(9849162151478227673)
XLA Ops:
  0.0 0.0 copy-start.2
  0.0 0.0 copy-start
  0.0 0.0 copy-start.1
  0.0 0.0 copy-start.3
  0.0 0.7 copy-done.2
  0.7 0.0 copy-done
  0.7 0.0 copy-done.1
  0.7 0.0 copy-done.3
  0.7 66.7 %propagate.1 = f32[1024,128]{1,0:T(8,128)S(1)} custom-call(f32[1024,128]{1,0:T(8,128)} %bitcast.15, f32[2,256,256]{2,1,0:T(8,128)} %prop_hbm.1, s32[2,8]{1,0:T(2,128)S(1)} %copy-done.1, f32[3,16]{1,0:T(4,128)S(1)} %copy-done, s32[2,32]{1,0:T(2,128)S(1)} %bitcast.13, f32[1,32]{1,0:T(1,128)S(1)} %bitcast.14), custom_call_target="tpu_custom_call" | custom-call | tf_op jit(solution)/shard_map/propagate/pallas_call | solution.py:650
  67.4 0.8 %copy.10 = f32[8,2,16,2,256]{4,3,2,1,0:T(2,128)} copy(f32[8,2,16,2,256]{4,3,2,1,0:T(2,128)S(1)} %bitcast.12) | data formatting | bytes 1048576
Async XLA Ops:
  0.0 0.7 copy-start.2
  0.0 0.7 %copy-start = (f32[3,16]{1,0:T(4,128)S(1)}, f32[3,16]{1,0:T(4,128)}, u32[]{:S(2)}) copy-start(f32[3,16]{1,0:T(4,128)} %cent_hbm.1) | copy-start | bytes 580
  0.0 0.7 %copy-start.1 = (s32[2,8]{1,0:T(2,128)S(1)}, s32[2,8]{1,0:T(2,128)}, u32[]{:S(2)}) copy-start(s32[2,8]{1,0:T(2,128)} %len_hbm.1) | copy-start | bytes 196
  0.0 0.7 %copy-start.3 = (f32[32]{0:T(128)S(1)}, f32[32]{0:T(128)}, u32[]{:S(2)}) copy-start(f32[32]{0:T(128)} %param.11) | copy-start | bytes 388

commit v7 on v5

--- a/solution.py
+++ b/solution.py
@@ -483,8 +483,8 @@
         arrived(hbuf, 0, 2, NS)
         z = second_pair([hbuf[0, :, i3].reshape(N, 128) for i3 in range(L3)])
         for i3 in range(L3):
-            gbuf[0, :, i3] = flip_blocks(z[i3].reshape(NP, 8, 128))
-        pencil_exchange(gbuf, rbuf, 0, 3)
+            gbuf[i3] = flip_blocks(z[i3].reshape(NP, 8, 128))
+            pencil_exchange(gbuf, rbuf, i3, 3 + 9 * i3)
 
     def edge_potential(psi, chunk):
         turned = psi * cos_e[chunk] + sin_e[chunk] * pltpu.roll(psi, 64, 1)
@@ -528,10 +528,10 @@
     r = [jnp.stack([e_rbuf[chunk, :, i3] for chunk in range(CHUNKS)], axis=1).reshape(N, 128) for i3 in range(L3)]
     wf = [(wf_hi[k], wf_lo[k]) for k in range(2)]
     early = [product(split2(a.T), wf[1]) for a in r]
-    arrived(rbuf, 0, 3, NP)
     block = (kron_hi[:128, :128], kron_lo[:128, :128])
     for i3 in range(L3):
-        out = early[i3] + product(split2(rbuf[0, :, i3].reshape(N, 128).T), wf[0])
+        arrived(rbuf, i3, 3 + 9 * i3, NP)
+        out = early[i3] + product(split2(rbuf[i3].reshape(N, 128).T), wf[0])
         out = potential(out[:, :N], out[:, N:], block, i3 * L2, L2)
         for part in range(2):
             for i2 in range(L2):
@@ -543,6 +543,7 @@
     left(sbuf, 0, 1, NS)
     left(ebuf, 0, 2, NS)
     left(gbuf, 0, 3, NP)
+    left(gbuf, 1, 12, NP)
     for chunk in range(CHUNKS):
         left(e_ybuf, chunk, 4 + chunk, NS)
         left(e_kbuf, chunk, 6 + chunk, NP)
@@ -606,8 +607,8 @@
         vmem(1, NS, L3, 16, 128),
         vmem(1, NS, L3, 16, 128),
         vmem(1, NS, L3, 16, 128),
-        vmem(1, NP, L3, 8, 128),
-        vmem(1, NP, L3, 8, 128),
+        vmem(L3, NP, 8, 128),
+        vmem(L3, NP, 8, 128),
         vmem(CHUNKS, N, 128),
         vmem(CHUNKS, N, 128),
         vmem(CHUNKS, N, 128),
@@ -623,8 +624,8 @@
         vmem(CHUNKS, NS, L3, 8, 128),
         vmem(CHUNKS, NS, L3, 8, 128),
         pltpu.SemaphoreType.DMA((6,)),
-        pltpu.SemaphoreType.DMA((12,)),
-        pltpu.SemaphoreType.DMA((12,)),
+        pltpu.SemaphoreType.DMA((13,)),
+        pltpu.SemaphoreType.DMA((13,)),
         pltpu.SemaphoreType.DMA((5,)),
         pltpu.SemaphoreType.DMA((5,)),
     ]

time: 68.5 us -> 68.4 us (level)
  no operation moved by 1% of the time
where the time goes in v7:
time: 68.4 us; the launch traced here: 68.3 us
  Pallas kernels  66.8 us (98%)
  local copies, waits for them, and re-layouts  1.5 us (2%)
    pallas_call x1, Pallas kernels, on_device(): pl.pallas_call(body, out_shape=jax.ShapeDtypeStruct((1024, 128), F32), in...  66.8 us
    unnamed x9, local copies, waits for them, and re-layouts  1.5 us

profile of v7, /device:TPU:1, one launch (start us, length us, event | category | flops | bytes accessed | tf_op | source)
XLA Modules:
  0.0 68.3 jit_solution(17594464623220192570)
XLA Ops:
  0.0 0.0 copy-start.2
  0.0 0.0 copy-start
  0.0 0.0 copy-start.1
  0.0 0.0 copy-start.3
  0.0 0.7 copy-done.2
  0.7 0.0 copy-done
  0.7 0.0 copy-done.1
  0.7 0.0 copy-done.3
  0.7 66.8 %propagate.1 = f32[1024,128]{1,0:T(8,128)S(1)} custom-call(f32[1024,128]{1,0:T(8,128)} %bitcast.15, f32[2,256,256]{2,1,0:T(8,128)} %prop_hbm.1, s32[2,8]{1,0:T(2,128)S(1)} %copy-done.1, f32[3,16]{1,0:T(4,128)S(1)} %copy-done, s32[2,32]{1,0:T(2,128)S(1)} %bitcast.13, f32[1,32]{1,0:T(1,128)S(1)} %bitcast.14), custom_call_target="tpu_custom_call" | custom-call | tf_op jit(solution)/shard_map/propagate/pallas_call | solution.py:632
  67.5 0.8 %copy.10 = f32[8,2,16,2,256]{4,3,2,1,0:T(2,128)} copy(f32[8,2,16,2,256]{4,3,2,1,0:T(2,128)S(1)} %bitcast.12) | data formatting | bytes 1048576
Async XLA Ops:
  0.0 0.7 copy-start.2
  0.0 0.7 %copy-start = (f32[3,16]{1,0:T(4,128)S(1)}, f32[3,16]{1,0:T(4,128)}, u32[]{:S(2)}) copy-start(f32[3,16]{1,0:T(4,128)} %cent_hbm.1) | copy-start | bytes 580
  0.0 0.7 %copy-start.1 = (s32[2,8]{1,0:T(2,128)S(1)}, s32[2,8]{1,0:T(2,128)}, u32[]{:S(2)}) copy-start(s32[2,8]{1,0:T(2,128)} %len_hbm.1) | copy-start | bytes 196
  0.0 0.7 %copy-start.3 = (f32[32]{0:T(128)S(1)}, f32[32]{0:T(128)}, u32[]{:S(2)}) copy-start(f32[32]{0:T(128)} %param.11) | copy-start | bytes 388
